TPU v7x, 32 devices: a whole 2x2x4 slice. The times are simulated.
32 devices in a mesh: section: 4 (over y, x), expert: 8 (over z, core).
Axes of the slice: x: 2, y: 2, z: 4, core: 2. Of those that a mesh axis runs over, the one named last changes fastest.
Arguments:
- tokens_a: bfloat16 [128, 3584], P('expert'), may hold values from -6 to 6
- routes_a: int32 [128, 8], P('expert'), may hold values from 0 to 7, as said below
- gates_a: float32 [128, 8], P('expert'), may hold values from 0.1 to 0.4
- cotangent_b: bfloat16 [128, 3584], P('expert'), may hold values from -6 to 6
- routes_b: int32 [128, 8], P('expert'), may hold values from 0 to 7, as said below
- gates_b: float32 [128, 8], P('expert'), may hold values from 0.1 to 0.4
- gate_weight: bfloat16 [8, 3584, 2048], P('expert', None, 'section'), may hold values from -0.09375 to 0.09375
- up_weight: bfloat16 [8, 3584, 2048], P('expert', None, 'section'), may hold values from -0.09375 to 0.09375
- down_weight: bfloat16 [8, 2048, 3584], P('expert', 'section'), may hold values from -0.125 to 0.125
- saved_gate: bfloat16 [8, 128, 2048], P('expert', None, 'section'), may hold values from -6 to 6
- saved_up: bfloat16 [8, 128, 2048], P('expert', None, 'section'), may hold values from -6 to 6
Outputs:
- forward_out: bfloat16 [128, 3584], P('expert', 'section')
- input_grad: bfloat16 [128, 3584], P('expert', 'section')
Inputs may be any that keep to these rules, and one draw needn't show every extreme that they name: `routes_a`: each row names 8 different experts. Within each aligned block of 16 rows no expert is named more than 16 times, and one expert, the same in every block, is named exactly 16 times in each block. `routes_b`: each row names 8 different experts. Within each aligned block of 16 rows no expert is named more than 16 times, and one expert, the same in every block, is named exactly 16 times in each block.
All inputs are finite; a program needn't handle non-finite values.
Results may differ from a plain program's by a relative error of at most 0.015.
Values may be sent and summed in bfloat16 or wider, within the bound.
No kernel may reach another device: no remote copies, remote signals or barrier semaphores. Data moves between devices by JAX's collectives and lax.ppermute only.
A program may use at most 64 MiB of HBM per device.

v0:
```python
import functools

import jax
import jax.numpy as jnp
from jax import lax
from jax.experimental import pallas as pl
from jax.experimental.pallas import tpu as pltpu
from jax.sharding import PartitionSpec as P

LANES = 128
CONTRACT_LAST = (((1,), (1,)), ((), ()))


def route_slots(routes, experts, capacity):
    flat_ids = routes.reshape(-1)
    onehot = (flat_ids[:, None] == jnp.arange(experts, dtype=jnp.int32)[None, :]).astype(jnp.int32)
    before = jnp.cumsum(onehot, axis=0) - onehot
    ranking = jnp.sum(before * onehot, axis=1)
    return flat_ids * capacity + ranking


def fill_slots(values, slot_index, slot_total):
    return jnp.zeros((slot_total, values.shape[1]), values.dtype).at[slot_index].set(values)


def routed_body(
    tokens_a,
    routes_a,
    gates_a,
    cotangent_b,
    routes_b,
    gates_b,
    gate_weight,
    up_weight,
    down_weight,
    saved_gate,
    saved_up,
):
    experts = lax.axis_size("expert")
    sections = lax.axis_size("section")
    token_count, feature_count = tokens_a.shape
    top_count = routes_a.shape[1]
    slot_count = saved_gate.shape[1]
    capacity = slot_count // experts
    column_count = feature_count // sections
    offset = lax.axis_index("section") * column_count
    where_a = route_slots(routes_a, experts, capacity)
    where_b = route_slots(routes_b, experts, capacity)
    values_a = jnp.repeat(tokens_a, top_count, axis=0)
    repeated_b = jnp.repeat(cotangent_b, top_count, axis=0)
    gate_col = gates_b.reshape(-1, 1)
    slice_a = lax.dynamic_slice_in_dim(values_a, offset, column_count, 1)
    slice_b = lax.dynamic_slice_in_dim(repeated_b, offset, column_count, 1)
    slice_b = (gate_col * slice_b.astype(jnp.float32)).astype(jnp.bfloat16)
    send_a = fill_slots(slice_a, where_a, slot_count).reshape(experts, capacity, column_count)
    send_b = fill_slots(slice_b, where_b, slot_count).reshape(experts, capacity, column_count)
    got_a, got_b = (
        lax.all_to_all(send_a, "expert", split_axis=0, concat_axis=0, tiled=True),
        lax.all_to_all(send_b, "expert", split_axis=0, concat_axis=0, tiled=True),
    )
    recv_a, recv_b = (
        lax.all_gather(got_a, "section", axis=2, tiled=True),
        lax.all_gather(got_b, "section", axis=2, tiled=True),
    )
    rows_a = recv_a.reshape(slot_count, feature_count)
    rows_b = recv_b.reshape(slot_count, feature_count)
    w_gate = gate_weight[0]
    w_up = up_weight[0]
    w_down = down_weight[0]
    gate_pre = jnp.dot(rows_a, w_gate, preferred_element_type=jnp.float32)
    up_pre = jnp.dot(rows_a, w_up, preferred_element_type=jnp.float32)
    hidden = (jax.nn.silu(gate_pre) * up_pre).astype(jnp.bfloat16)
    part_y = jnp.dot(hidden, w_down, preferred_element_type=jnp.float32)
    grad_hidden = lax.dot_general(
        rows_b, w_down, (((1,), (1,)), ((), ())), preferred_element_type=jnp.float32
    )
    pre_gate = saved_gate[0].astype(jnp.float32)
    pre_up = saved_up[0].astype(jnp.float32)
    squash = jax.nn.sigmoid(pre_gate)
    grad_up = (grad_hidden * (pre_gate * squash)).astype(jnp.bfloat16)
    grad_gate = (grad_hidden * pre_up * squash * (1.0 + pre_gate * (1.0 - squash))).astype(
        jnp.bfloat16
    )
    contract = (((1,), (1,)), ((), ()))
    part_dx = lax.dot_general(grad_gate, w_gate, contract, preferred_element_type=jnp.float32)
    part_dx = part_dx + lax.dot_general(grad_up, w_up, contract, preferred_element_type=jnp.float32)
    summed_y, summed_dx = (
        lax.psum_scatter(
            part_y.astype(jnp.bfloat16), "section", scatter_dimension=1, tiled=True
        ).astype(jnp.float32),
        lax.psum_scatter(
            part_dx.astype(jnp.bfloat16), "section", scatter_dimension=1, tiled=True
        ).astype(jnp.float32),
    )
    out_y = summed_y.astype(jnp.bfloat16).reshape(experts, capacity, column_count)
    out_dx = summed_dx.astype(jnp.bfloat16).reshape(experts, capacity, column_count)
    back_y, back_dx = (
        lax.all_to_all(out_y, "expert", split_axis=0, concat_axis=0, tiled=True),
        lax.all_to_all(out_dx, "expert", split_axis=0, concat_axis=0, tiled=True),
    )
    returned_y = back_y.reshape(slot_count, column_count)[where_a].reshape(
        token_count, top_count, column_count
    )
    returned_dx = back_dx.reshape(slot_count, column_count)[where_b].reshape(
        token_count, top_count, column_count
    )
    forward_out = jnp.sum(gates_a[:, :, None] * returned_y.astype(jnp.float32), axis=1).astype(
        jnp.bfloat16
    )
    input_grad = jnp.sum(returned_dx.astype(jnp.float32), axis=1).astype(jnp.bfloat16)
    return (forward_out, input_grad)


def call(kernel, outs, args, scratch=(), limit=8 << 20, cost=None, far=(), after=()):
    shapes = [jax.ShapeDtypeStruct(shape, dtype) for shape, dtype in outs]
    return pl.pallas_call(
        kernel,
        out_shape=shapes,
        in_specs=[
            pl.BlockSpec(
                memory_space=pltpu.HBM if i in far else pl.ANY if i in after else pltpu.VMEM
            )
            for i in range(len(args))
        ],
        out_specs=[pl.BlockSpec(memory_space=pltpu.VMEM)] * len(outs),
        scratch_shapes=list(scratch),
        compiler_params=pltpu.CompilerParams(vmem_limit_bytes=limit),
        cost_estimate=cost,
    )(*[pltpu.with_memory_space_constraint(x, pltpu.HBM) if i in far else x for i, x in enumerate(args)])


def columns(index, width):
    return pl.ds(pl.multiple_of(index * width, LANES), width)


def section_mask(step, steps, core):
    return jnp.where(core == 0, 1 << step, 1 << (steps - 1 - step))


def section_of(index, steps, section, core):
    for k in range(steps):
        if index >> k & 1:
            section = section ^ section_mask(k, steps, core)
    return section


def reverse_bits(index, steps):
    return sum((index >> k & 1) << (steps - 1 - k) for k in range(steps))


def swap_expert(x, mask):
    size = lax.axis_size("expert")
    return lax.ppermute(x, "expert", [(i, i ^ mask) for i in range(size)])


def swap_section(x, mask):
    size = lax.axis_size("section")
    return lax.ppermute(x, "section", [(i, i ^ mask) for i in range(size)])


def swap_halves(x, step, steps):
    experts = lax.axis_size("expert")
    sections = lax.axis_size("section")
    pairs = []
    for s in range(sections):
        for e in range(experts):
            mask = 1 << (step if e & 1 == 0 else steps - 1 - step)
            pairs.append((s * experts + e, (s ^ mask) * experts + e))
    return lax.ppermute(x, ("section", "expert"), pairs)


def gate_table(routes, gates, experts):
    parts = []
    for m in range(2):
        by_expert = jnp.concatenate(
            [
                jnp.sum(jnp.where(routes[m] == e, gates[m], 0.0), axis=0, keepdims=True)
                for e in range(experts)
            ],
            axis=0,
        )
        high = by_expert.astype(jnp.bfloat16).astype(jnp.float32)
        parts += [high, (by_expert - high).astype(jnp.bfloat16).astype(jnp.float32)]
    parts = jnp.concatenate(parts, axis=0)
    row = lax.broadcasted_iota(jnp.int32, (4 * experts, LANES), 0)
    col = lax.broadcasted_iota(jnp.int32, (4 * experts, LANES), 1)
    place = (row == col).astype(jnp.bfloat16)
    table = lax.dot_general(
        parts.T.astype(jnp.bfloat16),
        place,
        (((1,), (0,)), ((), ())),
        preferred_element_type=jnp.float32,
    )
    return table.astype(jnp.bfloat16)


def prepare_kernel(experts, width, xa, ra, ga, xb, rb, gb, full, sent, *scratch):
    routes, gates, sem = scratch
    features = xa.shape[1]
    small, large = [], []
    for m, (x, r, g) in enumerate(((xa, ra, ga), (xb, rb, gb))):
        small.append(pltpu.make_async_copy(r, routes.at[m], sem.at[3 * m]))
        small.append(pltpu.make_async_copy(g, gates.at[m], sem.at[3 * m + 1]))
        target = full.at[:, pl.ds(m * features, features)]
        large.append(pltpu.make_async_copy(x, target, sem.at[3 * m + 2]))
    for copy in (*small, *large):
        copy.start()
    for copy in small:
        copy.wait()
    table = gate_table(routes, gates, experts)
    full[:, 2 * features :] = table
    sent[:, 2 * width :] = table
    section = lax.axis_index("section")
    for m in range(2):
        large[m].wait()
        where = pl.ds(pl.multiple_of(m * features + section * width, LANES), width)
        sent[:, m * width : (m + 1) * width] = full[:, where]


def start_chunks(source, target, axis, chunk, sem, first):
    copies = []
    for i in range(source.shape[axis] // chunk):
        where = pl.ds(i * chunk, chunk)
        at = (slice(None), where) if axis else (where, slice(None))
        copies.append(pltpu.make_async_copy(source.at[at], target.at[at], sem.at[first + i]))
        copies[-1].start()
    return copies


def turn_chunks(copies, source, target, axis, chunk):
    for i, copy in enumerate(copies):
        copy.wait()
        where = pl.ds(i * chunk, chunk)
        if axis:
            target[where, :] = source[:, where].T
        else:
            target[:, where] = source[where, :].T


def load_kernel(experts, chunk, down, gate, saved_gate, saved_up, _, *refs):
    kept_down, kept_gate, turned_down, turned_gate, up_factor, gate_factor, saved, sem = refs
    count = down.shape[1] // chunk
    rows = []
    for n, source in enumerate((saved_gate, saved_up)):
        rows.append(pltpu.make_async_copy(source, saved.at[n], sem.at[2 * count + n]))
    for copy in rows:
        copy.start()
    down_copies = start_chunks(down, kept_down, 1, chunk, sem, 0)
    gate_copies = start_chunks(gate, kept_gate, 0, chunk, sem, count)
    for copy in rows:
        copy.wait()
    expert = lax.axis_index("expert")
    tokens = saved.shape[1] // experts
    for side in range(2):
        for d in range(experts // 2):
            block = expert ^ (2 * d + side)
            source = pl.ds(pl.multiple_of(block * tokens, tokens), tokens)
            target = pl.ds((side * (experts // 2) + d) * tokens, tokens)
            pre_gate = saved[0, source].astype(jnp.float32)
            pre_up = saved[1, source].astype(jnp.float32)
            squash = 1.0 / (1.0 + jnp.exp(-pre_gate))
            up_factor[target] = pre_gate * squash
            gate_factor[target] = pre_up * squash * (1.0 + pre_gate * (1.0 - squash))
    turn_chunks(down_copies, kept_down, turned_down, 1, chunk)
    turn_chunks(gate_copies, kept_gate, turned_gate, 0, chunk)


def load_last_kernel(chunk, weight, _, kept, turned, sem):
    copies = start_chunks(weight, kept, 0, chunk, sem, 0)
    turn_chunks(copies, kept, turned, 0, chunk)


def join_kernel(width, *refs):
    *parts, _, _, joined, sent_a, sent_b = refs
    rows = parts[0].shape[0]
    for i, part in enumerate(parts):
        where = slice(i * rows, (i + 1) * rows)
        joined[where] = part[...]
        sent_a[where] = part[:, :width]
        sent_b[where] = part[:, width : 2 * width]


def stack_kernel(count, *refs):
    parts, out = refs[:count], refs[-1]
    at = 0
    for part in parts:
        if len(part.shape) == 2:
            out[at] = part[...]
            at += 1
        else:
            out[at : at + part.shape[0]] = part[...]
            at += part.shape[0]


def assemble(m, width, sides, section_of_piece, rows_ref, table_ref):
    half = rows_ref.shape[0] // 2
    features = rows_ref.shape[1]
    for side, (full, joined, got) in enumerate(sides):
        tokens = full.shape[0]
        base = side * half
        rows_ref[base : base + tokens] = full[:, m * features : (m + 1) * features]
        table_ref[base : base + tokens] = full[:, 2 * features :]
        table_ref[base + tokens : base + half] = joined[:, 2 * width :]
        pieces = [joined[:, m * width : (m + 1) * width], *[piece[...] for piece in got]]
        for i, piece in enumerate(pieces):
            rows_ref[base + tokens : base + half, columns(section_of_piece(i, side), width)] = piece


def sent_order(sections):
    return [sections - 1, *range(1, sections - 1)]


def scale_column(m, experts, table_ref):
    first = 2 * m * experts + lax.axis_index("expert")
    table = table_ref[...].astype(jnp.float32)
    lane = lax.broadcasted_iota(jnp.int32, table.shape, 1)
    mine = (lane == first) | (lane == first + experts)
    return jnp.sum(jnp.where(mine, table, 0.0), axis=1, keepdims=True)


def store_pieces(sections, width, product, own, sibling):
    steps = sections.bit_length() - 1
    section = lax.axis_index("section")
    core = lax.axis_index("expert") & 1
    half = own.shape[1]
    size = sections * width
    block = 4 * LANES if size % (4 * LANES) == 0 else width
    for start in range(0, size, block):
        part = product(pl.ds(start, block)).astype(own.dtype)
        for quarter in range(sections):
            low, high = max(start, quarter * width), min(start + block, (quarter + 1) * width)
            if low < high:
                index = section ^ quarter
                turned = reverse_bits(index, steps)
                here = slice(low - start, high - start)
                there = pl.ds(low - quarter * width, high - low)
                own[jnp.where(core == 0, index, turned), :, there] = part[:half, here]
                sibling[jnp.where(core == 0, turned, index), :, there] = part[half:, here]


def forward_kernel(experts, sections, width, *refs):
    full, joined, stacked, sib_full, sib_joined, sib_stacked = refs[:6]
    w_down, w_gate, w_up, _, *outs, rows_ref, table_ref = refs[6:]
    section = lax.axis_index("section")
    core = lax.axis_index("expert") & 1
    sides = [
        (x, y, [z.at[i] for i in range(sections - 1)])
        for x, y, z in ((full, joined, stacked), (sib_full, sib_joined, sib_stacked))
    ]
    steps = sections.bit_length() - 1
    assemble(
        0,
        width,
        sides,
        lambda i, side: section_of(i, steps, section, core ^ side),
        rows_ref,
        table_ref,
    )
    scale = scale_column(0, experts, table_ref)
    rows = rows_ref[...]
    gate_pre = jnp.dot(rows, w_gate[...], preferred_element_type=jnp.float32)
    up_pre = jnp.dot(rows, w_up[...], preferred_element_type=jnp.float32)
    hidden = gate_pre / (1.0 + jnp.exp(-gate_pre)) * up_pre * scale
    hidden = hidden.astype(jnp.bfloat16)

    def product(where):
        return jnp.dot(hidden, w_down[:, where], preferred_element_type=jnp.float32)

    store_pieces(sections, width, product, *outs)


def backward_kernel(experts, sections, width, *refs):
    full, joined, *got = refs[: 1 + sections]
    sib_full, sib_joined, first, last = refs[1 + sections : 5 + sections]
    w_down, w_gate, w_up, up_factor, gate_factor, *outs, rows_ref, table_ref = refs[5 + sections :]
    section = lax.axis_index("section")
    order = sent_order(sections)
    sib_got = [last.at[0] if d == order[-1] else first.at[order.index(d)] for d in range(1, sections)]
    sides = [(full, joined, got), (sib_full, sib_joined, sib_got)]
    assemble(1, width, sides, lambda i, side: section ^ i, rows_ref, table_ref)
    scale = scale_column(1, experts, table_ref)
    grad_hidden = scale * jnp.dot(
        rows_ref[...], w_down[...], preferred_element_type=jnp.float32
    )
    grad_up = (grad_hidden * up_factor[...]).astype(jnp.bfloat16)
    grad_gate = (grad_hidden * gate_factor[...]).astype(jnp.bfloat16)

    def product(where):
        part = jnp.dot(grad_gate, w_gate[:, where], preferred_element_type=jnp.float32)
        return part + jnp.dot(grad_up, w_up[:, where], preferred_element_type=jnp.float32)

    store_pieces(sections, width, product, *outs)


def sum_kernel(count, starts, *refs):
    parts, outs = refs[:count], refs[-len(starts) :]
    for at, out in zip(starts, outs):
        where = slice(at, at + out.shape[0])
        total = parts[0][where].astype(jnp.float32)
        for part in parts[1:]:
            total = total + part[where].astype(jnp.float32)
        out[...] = total.astype(out.dtype)


def low_sum_kernel(own_a, got_a, own_b, got_b, _, out):
    for m, (own, got) in enumerate(((own_a, got_a), (own_b, got_b))):
        out[m] = (own[2].astype(jnp.float32) + got[2].astype(jnp.float32)).astype(out.dtype)


def block_sum_kernel(*refs):
    parts, got_low, outs = (refs[:2], refs[2:4]), refs[4], refs[5:]
    for m in range(2):
        total = got_low[m].astype(jnp.float32)
        for part in parts[m]:
            total = total + part[0].astype(jnp.float32)
        rows = outs[0].shape[1]
        for i, out in enumerate(outs):
            out[m] = total[i * rows : (i + 1) * rows].astype(out.dtype)


def final_sum_kernel(*refs):
    *parts, out_a, out_b = refs
    for m, out in enumerate((out_a, out_b)):
        total = parts[0][m].astype(jnp.float32)
        for part in parts[1:]:
            total = total + part[m].astype(jnp.float32)
        out[...] = total.astype(out.dtype)


def dense_body(
    tokens_a,
    routes_a,
    gates_a,
    cotangent_b,
    routes_b,
    gates_b,
    gate_weight,
    up_weight,
    down_weight,
    saved_gate,
    saved_up,
):
    experts = lax.axis_size("expert")
    sections = lax.axis_size("section")
    steps = sections.bit_length() - 1
    token_count, feature_count = tokens_a.shape
    hidden_count = gate_weight.shape[2]
    slot_count = saved_gate.shape[1]
    width = feature_count // sections
    half = slot_count // 2
    chunk = width
    far_tokens = half - token_count
    dtype = tokens_a.dtype
    cost = pl.CostEstimate(
        flops=6 * slot_count * feature_count * hidden_count,
        bytes_accessed=6 * feature_count * hidden_count,
        transcendentals=slot_count * hidden_count,
    )
    long = pl.CostEstimate(flops=60 * slot_count * feature_count * hidden_count, bytes_accessed=0, transcendentals=0)
    quick = pl.CostEstimate(flops=1000, bytes_accessed=1000, transcendentals=0)
    def stack(parts, cost, after=()):
        count = sum(1 if x.ndim == 2 else x.shape[0] for x in parts)
        return call(
            functools.partial(stack_kernel, len(parts)),
            [((count, far_tokens, width), dtype)],
            [*parts, *after],
            cost=cost,
            after=range(len(parts), len(parts) + len(after)),
        )[0]

    full, sent = call(
        functools.partial(prepare_kernel, experts, width),
        [
            ((token_count, 2 * feature_count + LANES), dtype),
            ((token_count, 2 * width + LANES), dtype),
        ],
        [tokens_a, routes_a.T, gates_a.T, cotangent_b, routes_b.T, gates_b.T],
        [
            pltpu.VMEM((2, *routes_a.shape[::-1]), routes_a.dtype),
            pltpu.VMEM((2, *gates_a.shape[::-1]), gates_a.dtype),
            pltpu.SemaphoreType.DMA((6,)),
        ],
        far=range(6),
    )
    sib_full = swap_expert(full, 1)
    parts = [swap_expert(sent, 2 * d) for d in reversed(range(1, experts // 2))][::-1]
    weight_shape = ((feature_count, hidden_count), dtype)
    turned_shape = ((hidden_count, feature_count), dtype)
    factor = ((slot_count, hidden_count), jnp.float32)
    loaded = call(
        functools.partial(load_kernel, experts, chunk),
        [turned_shape, weight_shape, weight_shape, turned_shape, factor, factor],
        [down_weight[0], gate_weight[0], saved_gate[0], saved_up[0], sent],
        [
            pltpu.VMEM((2, slot_count, hidden_count), dtype),
            pltpu.SemaphoreType.DMA((2 * (feature_count // chunk) + 2,)),
        ],
        cost=cost,
        far=range(4),
        after=[4],
    )
    weights, turned, factors = loaded[:2], loaded[2:4], loaded[4:]
    piece = ((far_tokens, width), dtype)
    joined, sent_a, sent_b = call(
        functools.partial(join_kernel, width),
        [((far_tokens, 2 * width + LANES), dtype), piece, piece],
        [*parts, turned[0], sib_full],
        after=[len(parts), len(parts) + 1],
    )
    sib_joined = swap_expert(joined, 1)
    order = sent_order(sections)
    arrived = {d: swap_section(sent_b, d) for d in order}
    got_b = [arrived[d] for d in range(1, sections)]
    got_a = [swap_halves(sent_a, 0, steps)]
    for k in range(1, steps):
        early = stack([sent_a, *got_a], quick)
        got_a.append(swap_halves(early, k, steps))
    out = ((sections, half, width), dtype)
    scratch = [
        pltpu.VMEM((slot_count, feature_count), dtype),
        pltpu.VMEM((slot_count, LANES), dtype),
    ]
    def compute(kernel, args, after=()):
        return call(
            functools.partial(kernel, experts, sections, width),
            [out] * 2,
            [*args, *after],
            scratch,
            limit=16 << 20,
            cost=quick,
            after=range(len(args), len(args) + len(after)),
        )

    def add(parts, counts, cost, after=()):
        starts, at = [], 0
        for n in counts:
            if n is not None:
                starts.append(at)
            at += 1 if n is None else n
        return call(
            functools.partial(sum_kernel, len(parts), starts),
            [((n, half, width), dtype) for n in counts if n is not None],
            [*parts, *after],
            cost=cost,
            after=range(len(parts), len(parts) + len(after)),
        )

    last_weight, last_turned = call(
        functools.partial(load_last_kernel, chunk),
        [weight_shape, turned_shape],
        [up_weight[0], early],
        [pltpu.SemaphoreType.DMA((feature_count // chunk,))],
        cost=quick,
        far=range(1),
        after=[1],
    )
    weights, turned = [*weights, last_weight], [*turned, last_turned]
    first = stack([arrived[d] for d in order[:-1]], long, [last_turned])
    last = stack([arrived[order[-1]]], long, [last_turned, sib_joined])
    sib_b = [swap_expert(x, 1) for x in (first, last)]
    args = [full, joined, *got_b, sib_full, sib_joined, *sib_b, *turned, *factors]
    own_b, other_b = compute(backward_kernel, args)
    stacked = stack(got_a, quick, sib_b)
    sib_stacked = swap_expert(stacked, 1)
    args = [full, joined, stacked, sib_full, sib_joined, sib_stacked, *weights]
    own_a, other_a = compute(forward_kernel, args, [own_b])
    partial = {}
    for m, own, other in (("b", own_b, other_b), ("a", own_a, other_a)):
        parts = [own, swap_expert(other, 1)]
        for k in reversed(range(2, steps)):
            kept, away = add(parts, [1 << k] * 2, quick)
            parts = [kept, swap_halves(away, k, steps)]
        partial[m] = parts
    high, near = {}, {}
    for m in ("b", "a"):
        *near[m], high[m] = add(partial[m], [1, 1, None, 1], quick)
    low = call(
        low_sum_kernel,
        [((2, half, width), dtype)],
        [*partial["a"], *partial["b"], high["a"]],
        cost=quick,
        after=[4],
    )[0]
    got_low = swap_halves(low, 1, steps)
    held = {}
    for m in ("b", "a"):
        kept, away = near[m]
        (away,) = add([away, swap_halves(high[m], 1, steps)], [1], quick)
        held[m] = [kept, swap_halves(away, 0, steps)]
    block = ((2, token_count, width), dtype)
    blocks = call(
        block_sum_kernel,
        [block] * (experts // 2),
        [*held["a"], *held["b"], got_low],
    )
    held = [blocks[0]] + [swap_expert(blocks[d], 2 * d) for d in reversed(range(1, experts // 2))]
    return call(final_sum_kernel, [((token_count, width), dtype)] * 2, held)


def power_of_two(n):
    return n & (n - 1) == 0


def body(*args):
    experts = lax.axis_size("expert")
    sections = lax.axis_size("section")
    token_count, feature_count = args[0].shape
    top_count = args[1].shape[1]
    dense = (
        top_count == experts
        and args[9].shape[1] == token_count * experts
        and power_of_two(experts)
        and power_of_two(sections)
        and experts > 2
        and sections.bit_length() == 3
        and 4 * experts <= LANES
        and token_count % 16 == 0
        and feature_count % (sections * LANES) == 0
    )
    return (dense_body if dense else routed_body)(*args)


def solution(mesh):
    placed = (
        P("expert", None),
        P("expert", None),
        P("expert", None),
        P("expert", None),
        P("expert", None),
        P("expert", None),
        P("expert", None, "section"),
        P("expert", None, "section"),
        P("expert", "section", None),
        P("expert", None, "section"),
        P("expert", None, "section"),
    )
    return jax.shard_map(
        body,
        mesh=mesh,
        in_specs=placed,
        out_specs=(P("expert", "section"), P("expert", "section")),
        check_vma=False,
    )
```

profile of v0, /device:TPU:0, one launch (start us, length us, event | category | flops | bytes accessed | tf_op | source)
XLA Modules:
  0.0 49.2 jit_solution(13698848357451623989)
XLA Ops:
  0.6 1.1 %shard_map.122 = (bf16[16,7296]{1,0:T(8,128)(2,1)S(1)}, bf16[16,1920]{1,0:T(8,128)(2,1)S(1)}) custom-call(bf16[16,3584]{1,0:T(8,128)(2,1)} %xa.1, s32[8,16]{1,0:T(8,128)} %bitcast.14, f32[8,16]{1,0:T(8,128)} %bitcast.15, bf16[16,3584]{1,0:T(8,128)(2,1)} %xb.1, s32[8,16]{1,0:T(8,128)} %bitcast.16, f32[8,16]{1,0:T(8,128)} %bitcast.17), custom_call_target="tpu_custom_call" | custom-call | tf_op jit(solution)/shard_map/pallas_call | solution.py:116
  1.7 0.5 %collective-permute-start.3 = (bf16[16,7296]{1,0:T(8,128)(2,1)S(1)}, bf16[16,7296]{1,0:T(8,128)(2,1)S(1)}, u32[]{:S(2)}, u32[]{:S(2)}) collective-permute-start(bf16[16,7296]{1,0:T(8,128)(2,1)S(1)} %get-tuple-element.29.refs_0_), channel_id=1, source_target_pairs={{0,1},{1,0},{2,3},{3,2},{4,5},{5,4},{6,7},{7,6},{8,9},{9,8},{10,11... | collective-permute-start | bytes 700424 | tf_op jit(solution)/shard_map/ppermute | solution.py:153
  2.2 4.7 %collective-permute-start.2 = (bf16[16,1920]{1,0:T(8,128)(2,1)S(1)}, bf16[16,1920]{1,0:T(8,128)(2,1)S(1)}, u32[]{:S(2)}, u32[]{:S(2)}) collective-permute-start(bf16[16,1920]{1,0:T(8,128)(2,1)S(1)} %get-tuple-element.30._), channel_id=1, source_target_pairs={{0,6},{1,7},{2,4},{3,5},{4,2},{5,3},{6,0},{7,1},{8,14},{9,15},{10,... | collective-permute-start | bytes 184328 | tf_op jit(solution)/shard_map/ppermute | solution.py:153
  6.9 0.6 %collective-permute-start = (bf16[16,1920]{1,0:T(8,128)(2,1)S(1)}, bf16[16,1920]{1,0:T(8,128)(2,1)S(1)}, u32[]{:S(2)}, u32[]{:S(2)}) collective-permute-start(bf16[16,1920]{1,0:T(8,128)(2,1)S(1)} %get-tuple-element.30._), channel_id=1, source_target_pairs={{0,2},{1,3},{2,0},{3,1},{4,6},{5,7},{6,4},{7,5},{8,10},{9,11},{10,... | collective-permute-start | bytes 184328 | tf_op jit(solution)/shard_map/ppermute | solution.py:153
  7.5 3.7 %shard_map.123 = (bf16[512,3584]{1,0:T(8,128)(2,1)S(1)}, bf16[3584,512]{1,0:T(8,128)(2,1)S(1)}, bf16[3584,512]{1,0:T(8,128)(2,1)S(1)}, bf16[512,3584]{1,0:T(8,12...) custom-call(bf16[512,3584]{1,0:T(8,128)(2,1)} %bitcast.9, bf16[3584,512]{1,0:T(8,128)(2,1)} %bitcast.10, ...), custom_call_target="tpu_custom_call" | custom-call | flops 1409286144 | bytes 11010048 | tf_op jit(solution)/shard_map/pallas_call | solution.py:116
  11.3 1.3 %collective-permute-done.1.refs_1_ = bf16[16,1920]{1,0:T(8,128)(2,1)S(1)} collective-permute-done((bf16[16,1920]{1,0:T(8,128)(2,1)S(1)}, bf16[16,1920]{1,0:T(8,128)(2,1)S(1)}, u32[]{:S(2)}, u32[]{:S(2)}) %collective-permute-start.1) | collective-permute-done | bytes 61472 | tf_op jit(solution)/shard_map/ppermute | solution.py:153
  12.7 1.6 %collective-permute-start.4 = (bf16[48,896]{1,0:T(8,128)(2,1)S(1)}, bf16[48,896]{1,0:T(8,128)(2,1)S(1)}, u32[]{:S(2)}, u32[]{:S(2)}) collective-permute-start(bf16[48,896]{1,0:T(8,128)(2,1)S(1)} %get-tuple-element.33.refs_0_), channel_id=1, source_target_pairs={{0,8},{1,17},{2,10},{3,19},{4,12},{5,21},{6,14},{7,23},{8,0},{9,25... | collective-permute-start | bytes 258056 | tf_op jit(solution)/shard_map/ppermute | solution.py:169
  14.2 0.5 %collective-permute-start.7 = (bf16[48,896]{1,0:T(8,128)(2,1)S(1)}, bf16[48,896]{1,0:T(8,128)(2,1)S(1)}, u32[]{:S(2)}, u32[]{:S(2)}) collective-permute-start(bf16[48,896]{1,0:T(8,128)(2,1)S(1)} %get-tuple-element.34), channel_id=1, source_target_pairs={{0,8},{8,0},{16,24},{24,16},{1,9},{9,1},{17,25},{25,17},{2,10},{10... | collective-permute-start | bytes 258056 | tf_op jit(solution)/shard_map/ppermute | solution.py:158
  14.8 2.4 %collective-permute-start.6 = (bf16[48,896]{1,0:T(8,128)(2,1)S(1)}, bf16[48,896]{1,0:T(8,128)(2,1)S(1)}, u32[]{:S(2)}, u32[]{:S(2)}) collective-permute-start(bf16[48,896]{1,0:T(8,128)(2,1)S(1)} %get-tuple-element.34), channel_id=1, source_target_pairs={{0,24},{8,16},{16,8},{24,0},{1,25},{9,17},{17,9},{25,1},{2,26},{10... | collective-permute-start | bytes 258056 | tf_op jit(solution)/shard_map/ppermute | solution.py:158
  17.2 0.5 %collective-permute-start.9 = (bf16[48,896]{1,0:T(8,128)(2,1)S(1)}, bf16[48,896]{1,0:T(8,128)(2,1)S(1)}, u32[]{:S(2)}, u32[]{:S(2)}) collective-permute-start(bf16[48,896]{1,0:T(8,128)(2,1)S(1)} %get-tuple-element.34), channel_id=1, source_target_pairs={{0,16},{8,24},{16,0},{24,8},{1,17},{9,25},{17,1},{25,9},{2,18},{10... | collective-permute-start | bytes 258056 | tf_op jit(solution)/shard_map/ppermute | solution.py:158
  18.0 1.3 %collective-permute-start.5 = (bf16[2,48,896]{2,1,0:T(8,128)(2,1)S(1)}, bf16[2,48,896]{2,1,0:T(8,128)(2,1)S(1)}, u32[]{:S(2)}, u32[]{:S(2)}) collective-permute-start(bf16[2,48,896]{2,1,0:T(8,128)(2,1)S(1)} %shard_map.125._), channel_id=1, source_target_pairs={{0,16},{1,9},{2,18},{3,11},{4,20},{5,13},{6,22},{7,15},{8,24},{9,1... | collective-permute-start | bytes 516104 | tf_op jit(solution)/shard_map/ppermute | solution.py:169
  19.3 2.4 %shard_map.126 = (bf16[3584,512]{1,0:T(8,128)(2,1)S(1)}, bf16[512,3584]{1,0:T(8,128)(2,1)S(1)}) custom-call(bf16[3584,512]{1,0:T(8,128)(2,1)} %bitcast.11, bf16[2,48,896]{2,1,0:T(8,128)(2,1)S(1)} %shard_map.125._), custom_call_target="tpu_custom_call" | custom-call | flops 1000 | bytes 1000 | tf_op jit(solution)/shard_map/pallas_call | solution.py:116
  21.8 0.4 collective-permute-done.9.refs_0_.refs_3_
  22.4 1.7 %collective-permute-done.5.refs_1_ = bf16[2,48,896]{2,1,0:T(8,128)(2,1)S(1)} collective-permute-done((bf16[2,48,896]{2,1,0:T(8,128)(2,1)S(1)}, bf16[2,48,896]{2,1,0:T(8,128)(2,1)S(1)}, u32[]{:S(2)}, u32[]{:S(2)}) %collective-permute-start.5) | collective-permute-done | bytes 172064 | tf_op jit(solution)/shard_map/ppermute | solution.py:169
  24.2 1.8 %shard_map.130 = (bf16[4,64,896]{2,1,0:T(8,128)(2,1)S(1)}, bf16[4,64,896]{2,1,0:T(8,128)(2,1)S(1)}) custom-call(bf16[16,7296]{1,0:T(8,128)(2,1)S(1)} %get-tuple-element.29.refs_0_, bf16[48,1920]{1,0:T(8,128)(2,1)S(1)} %get-tuple-element.32.refs_1_, bf16[48,896]{1,0:T(8,128)(2,1)S(1)} %collective-permute-done.7.refs_1_.refs_2_, ...), custom_call_target="tpu_custom_call" | custom-call | flops 1000 | bytes 1000 | tf_op jit(solution)/shard_map/pallas_call | solution.py:116
  26.0 0.6 %collective-permute-start.16 = (bf16[4,64,896]{2,1,0:T(8,128)(2,1)S(1)}, bf16[4,64,896]{2,1,0:T(8,128)(2,1)S(1)}, u32[]{:S(2)}, u32[]{:S(2)}) collective-permute-start(bf16[4,64,896]{2,1,0:T(8,128)(2,1)S(1)} %get-tuple-element.48), channel_id=1, source_target_pairs={{0,1},{1,0},{2,3},{3,2},{4,5},{5,4},{6,7},{7,6},{8,9},{9,8},{10,11... | collective-permute-start | bytes 1376264 | tf_op jit(solution)/shard_map/ppermute | solution.py:153
  26.6 1.8 %shard_map.131 = (bf16[4,64,896]{2,1,0:T(8,128)(2,1)S(1)}, bf16[4,64,896]{2,1,0:T(8,128)(2,1)S(1)}) custom-call(bf16[16,7296]{1,0:T(8,128)(2,1)S(1)} %get-tuple-element.29.refs_0_, bf16[48,1920]{1,0:T(8,128)(2,1)S(1)} %get-tuple-element.32.refs_1_, bf16[3,48,896]{2,1,0:T(8,128)(2,1)S(1)} %shard_map.129.refs_2_, ...), custom_call_target="tpu_custom_call" | custom-call | flops 1000 | bytes 1000 | tf_op jit(solution)/shard_map/pallas_call | solution.py:116
  28.5 1.1 %collective-permute-start.17 = (bf16[1,64,896]{2,1,0:T(8,128)(2,1)S(1)}, bf16[1,64,896]{2,1,0:T(8,128)(2,1)S(1)}, u32[]{:S(2)}, u32[]{:S(2)}) collective-permute-start(bf16[1,64,896]{2,1,0:T(8,128)(2,1)S(1)} %get-tuple-element.51), channel_id=1, source_target_pairs={{0,16},{1,9},{2,18},{3,11},{4,20},{5,13},{6,22},{7,15},{8,24},{9,1... | collective-permute-start | bytes 344072 | tf_op jit(solution)/shard_map/ppermute | solution.py:169
  29.6 0.6 %collective-permute-done.13.refs_1_.got_a = bf16[4,64,896]{2,1,0:T(8,128)(2,1)S(1)} collective-permute-done((bf16[4,64,896]{2,1,0:T(8,128)(2,1)S(1)}, bf16[4,64,896]{2,1,0:T(8,128)(2,1)S(1)}, u32[]{:S(2)}, u32[]{:S(2)}) %collective-permute-start.13) | collective-permute-done | bytes 458784 | tf_op jit(solution)/shard_map/ppermute | solution.py:153
  30.3 1.1 %collective-permute-start.14 = (bf16[1,64,896]{2,1,0:T(8,128)(2,1)S(1)}, bf16[1,64,896]{2,1,0:T(8,128)(2,1)S(1)}, u32[]{:S(2)}, u32[]{:S(2)}) collective-permute-start(bf16[1,64,896]{2,1,0:T(8,128)(2,1)S(1)} %get-tuple-element.47._), channel_id=1, source_target_pairs={{0,16},{1,9},{2,18},{3,11},{4,20},{5,13},{6,22},{7,15},{8,24},{9,1... | collective-permute-start | bytes 344072 | tf_op jit(solution)/shard_map/ppermute | solution.py:169
  31.5 1.1 %collective-permute-start.19 = (bf16[2,64,896]{2,1,0:T(8,128)(2,1)S(1)}, bf16[2,64,896]{2,1,0:T(8,128)(2,1)S(1)}, u32[]{:S(2)}, u32[]{:S(2)}) collective-permute-start(bf16[2,64,896]{2,1,0:T(8,128)(2,1)S(1)} %shard_map.136), channel_id=1, source_target_pairs={{0,16},{1,9},{2,18},{3,11},{4,20},{5,13},{6,22},{7,15},{8,24},{9,1... | collective-permute-start | bytes 688136 | tf_op jit(solution)/shard_map/ppermute | solution.py:169
  32.5 0.9 %collective-permute-done.17.refs_1_ = bf16[1,64,896]{2,1,0:T(8,128)(2,1)S(1)} collective-permute-done((bf16[1,64,896]{2,1,0:T(8,128)(2,1)S(1)}, bf16[1,64,896]{2,1,0:T(8,128)(2,1)S(1)}, u32[]{:S(2)}, u32[]{:S(2)}) %collective-permute-start.17) | collective-permute-done | bytes 114720 | tf_op jit(solution)/shard_map/ppermute | solution.py:169
  33.4 1.3 %collective-permute-start.18 = (bf16[1,64,896]{2,1,0:T(8,128)(2,1)S(1)}, bf16[1,64,896]{2,1,0:T(8,128)(2,1)S(1)}, u32[]{:S(2)}, u32[]{:S(2)}) collective-permute-start(bf16[1,64,896]{2,1,0:T(8,128)(2,1)S(1)} %shard_map.135), channel_id=1, source_target_pairs={{0,8},{1,17},{2,10},{3,19},{4,12},{5,21},{6,14},{7,23},{8,0},{9,25... | collective-permute-start | bytes 344072 | tf_op jit(solution)/shard_map/ppermute | solution.py:169
  34.8 0.4 collective-permute-done.14.refs_1_
  35.2 1.0 %collective-permute-start.15 = (bf16[1,64,896]{2,1,0:T(8,128)(2,1)S(1)}, bf16[1,64,896]{2,1,0:T(8,128)(2,1)S(1)}, u32[]{:S(2)}, u32[]{:S(2)}) collective-permute-start(bf16[1,64,896]{2,1,0:T(8,128)(2,1)S(1)} %shard_map.133), channel_id=1, source_target_pairs={{0,8},{1,17},{2,10},{3,19},{4,12},{5,21},{6,14},{7,23},{8,0},{9,25... | collective-permute-start | bytes 344072 | tf_op jit(solution)/shard_map/ppermute | solution.py:169
  36.2 2.1 %collective-permute-done.18.refs_3_ = bf16[1,64,896]{2,1,0:T(8,128)(2,1)S(1)} collective-permute-done((bf16[1,64,896]{2,1,0:T(8,128)(2,1)S(1)}, bf16[1,64,896]{2,1,0:T(8,128)(2,1)S(1)}, u32[]{:S(2)}, u32[]{:S(2)}) %collective-permute-start.18) | collective-permute-done | bytes 114720 | tf_op jit(solution)/shard_map/ppermute | solution.py:169
  38.3 1.8 %collective-permute-done.15.refs_1_ = bf16[1,64,896]{2,1,0:T(8,128)(2,1)S(1)} collective-permute-done((bf16[1,64,896]{2,1,0:T(8,128)(2,1)S(1)}, bf16[1,64,896]{2,1,0:T(8,128)(2,1)S(1)}, u32[]{:S(2)}, u32[]{:S(2)}) %collective-permute-start.15) | collective-permute-done | bytes 114720 | tf_op jit(solution)/shard_map/ppermute | solution.py:169
  40.2 2.4 %collective-permute-start.20 = (bf16[2,16,896]{2,1,0:T(8,128)(2,1)S(1)}, bf16[2,16,896]{2,1,0:T(8,128)(2,1)S(1)}, u32[]{:S(2)}, u32[]{:S(2)}) collective-permute-start(bf16[2,16,896]{2,1,0:T(8,128)(2,1)S(1)} %get-tuple-element.53), channel_id=1, source_target_pairs={{0,6},{1,7},{2,4},{3,5},{4,2},{5,3},{6,0},{7,1},{8,14},{9,15},{10,... | collective-permute-start | bytes 172040 | tf_op jit(solution)/shard_map/ppermute | solution.py:153
  42.8 1.9 %collective-permute-start.22 = (bf16[2,16,896]{2,1,0:T(8,128)(2,1)S(1)}, bf16[2,16,896]{2,1,0:T(8,128)(2,1)S(1)}, u32[]{:S(2)}, u32[]{:S(2)}) collective-permute-start(bf16[2,16,896]{2,1,0:T(8,128)(2,1)S(1)} %get-tuple-element.55), channel_id=1, source_target_pairs={{0,2},{1,3},{2,0},{3,1},{4,6},{5,7},{6,4},{7,5},{8,10},{9,11},{10,... | collective-permute-start | bytes 172040 | tf_op jit(solution)/shard_map/ppermute | solution.py:153
  44.6 2.1 %collective-permute-done.20.refs_1_ = bf16[2,16,896]{2,1,0:T(8,128)(2,1)S(1)} collective-permute-done((bf16[2,16,896]{2,1,0:T(8,128)(2,1)S(1)}, bf16[2,16,896]{2,1,0:T(8,128)(2,1)S(1)}, u32[]{:S(2)}, u32[]{:S(2)}) %collective-permute-start.20) | collective-permute-done | bytes 57376 | tf_op jit(solution)/shard_map/ppermute | solution.py:153
  46.7 1.9 %collective-permute-done.21.refs_2_ = bf16[2,16,896]{2,1,0:T(8,128)(2,1)S(1)} collective-permute-done((bf16[2,16,896]{2,1,0:T(8,128)(2,1)S(1)}, bf16[2,16,896]{2,1,0:T(8,128)(2,1)S(1)}, u32[]{:S(2)}, u32[]{:S(2)}) %collective-permute-start.21) | collective-permute-done | bytes 57376 | tf_op jit(solution)/shard_map/ppermute | solution.py:153
  48.6 0.6 %shard_map.138 = (bf16[16,896]{1,0:T(8,128)(2,1)}, bf16[16,896]{1,0:T(8,128)(2,1)}) custom-call(bf16[2,16,896]{2,1,0:T(8,128)(2,1)S(1)} %get-tuple-element.52.refs_0_, bf16[2,16,896]{2,1,0:T(8,128)(2,1)S(1)} %collective-permute-done.20.refs_1_, bf16[2,16,896]{2,1,0:T(8,128)(2,1)S(1)} %collective-permute-done.21.refs_2_, ...), custom_call_target="tpu_custom_call" | custom-call | tf_op jit(solution)/shard_map/pallas_call | solution.py:116
  (31 shorter events, 1.3 us)
Async XLA Ops:
  1.7 10.9 %collective-permute-start.3 = (bf16[16,7296]{1,0:T(8,128)(2,1)S(1)}, bf16[16,7296]{1,0:T(8,128)(2,1)S(1)}, u32[]{:S(2)}, u32[]{:S(2)}) collective-permute-start(bf16[16,7296]{1,0:T(8,128)(2,1)S(1)} %get-tuple-element.29.refs_0_), channel_id=1, source_target_pairs={{0,1},{1,0},{2,3},{3,2},{4,5},{5,4},{6,7},{7,6},{8,9},{9,8},{10,11... | collective-permute-start | bytes 700424 | tf_op jit(solution)/shard_map/ppermute | solution.py:153
  2.2 9.1 %collective-permute-start.2 = (bf16[16,1920]{1,0:T(8,128)(2,1)S(1)}, bf16[16,1920]{1,0:T(8,128)(2,1)S(1)}, u32[]{:S(2)}, u32[]{:S(2)}) collective-permute-start(bf16[16,1920]{1,0:T(8,128)(2,1)S(1)} %get-tuple-element.30._), channel_id=1, source_target_pairs={{0,6},{1,7},{2,4},{3,5},{4,2},{5,3},{6,0},{7,1},{8,14},{9,15},{10,... | collective-permute-start | bytes 184328 | tf_op jit(solution)/shard_map/ppermute | solution.py:153
  6.9 5.7 %collective-permute-start.1 = (bf16[16,1920]{1,0:T(8,128)(2,1)S(1)}, bf16[16,1920]{1,0:T(8,128)(2,1)S(1)}, u32[]{:S(2)}, u32[]{:S(2)}) collective-permute-start(bf16[16,1920]{1,0:T(8,128)(2,1)S(1)} %get-tuple-element.30._), channel_id=1, source_target_pairs={{0,4},{1,5},{2,6},{3,7},{4,0},{5,1},{6,2},{7,3},{8,12},{9,13},{10,... | collective-permute-start | bytes 184328 | tf_op jit(solution)/shard_map/ppermute | solution.py:153
  6.9 5.7 %collective-permute-start = (bf16[16,1920]{1,0:T(8,128)(2,1)S(1)}, bf16[16,1920]{1,0:T(8,128)(2,1)S(1)}, u32[]{:S(2)}, u32[]{:S(2)}) collective-permute-start(bf16[16,1920]{1,0:T(8,128)(2,1)S(1)} %get-tuple-element.30._), channel_id=1, source_target_pairs={{0,2},{1,3},{2,0},{3,1},{4,6},{5,7},{6,4},{7,5},{8,10},{9,11},{10,... | collective-permute-start | bytes 184328 | tf_op jit(solution)/shard_map/ppermute | solution.py:153
  12.7 5.3 %collective-permute-start.4 = (bf16[48,896]{1,0:T(8,128)(2,1)S(1)}, bf16[48,896]{1,0:T(8,128)(2,1)S(1)}, u32[]{:S(2)}, u32[]{:S(2)}) collective-permute-start(bf16[48,896]{1,0:T(8,128)(2,1)S(1)} %get-tuple-element.33.refs_0_), channel_id=1, source_target_pairs={{0,8},{1,17},{2,10},{3,19},{4,12},{5,21},{6,14},{7,23},{8,0},{9,25... | collective-permute-start | bytes 258056 | tf_op jit(solution)/shard_map/ppermute | solution.py:169
  14.2 7.5 %collective-permute-start.7 = (bf16[48,896]{1,0:T(8,128)(2,1)S(1)}, bf16[48,896]{1,0:T(8,128)(2,1)S(1)}, u32[]{:S(2)}, u32[]{:S(2)}) collective-permute-start(bf16[48,896]{1,0:T(8,128)(2,1)S(1)} %get-tuple-element.34), channel_id=1, source_target_pairs={{0,8},{8,0},{16,24},{24,16},{1,9},{9,1},{17,25},{25,17},{2,10},{10... | collective-permute-start | bytes 258056 | tf_op jit(solution)/shard_map/ppermute | solution.py:158
  14.8 7.0 %collective-permute-start.6 = (bf16[48,896]{1,0:T(8,128)(2,1)S(1)}, bf16[48,896]{1,0:T(8,128)(2,1)S(1)}, u32[]{:S(2)}, u32[]{:S(2)}) collective-permute-start(bf16[48,896]{1,0:T(8,128)(2,1)S(1)} %get-tuple-element.34), channel_id=1, source_target_pairs={{0,24},{8,16},{16,8},{24,0},{1,25},{9,17},{17,9},{25,1},{2,26},{10... | collective-permute-start | bytes 258056 | tf_op jit(solution)/shard_map/ppermute | solution.py:158
  17.2 5.1 %collective-permute-start.9 = (bf16[48,896]{1,0:T(8,128)(2,1)S(1)}, bf16[48,896]{1,0:T(8,128)(2,1)S(1)}, u32[]{:S(2)}, u32[]{:S(2)}) collective-permute-start(bf16[48,896]{1,0:T(8,128)(2,1)S(1)} %get-tuple-element.34), channel_id=1, source_target_pairs={{0,16},{8,24},{16,0},{24,8},{1,17},{9,25},{17,1},{25,9},{2,18},{10... | collective-permute-start | bytes 258056 | tf_op jit(solution)/shard_map/ppermute | solution.py:158
  17.7 4.6 %collective-permute-start.10 = (bf16[48,1920]{1,0:T(8,128)(2,1)S(1)}, bf16[48,1920]{1,0:T(8,128)(2,1)S(1)}, u32[]{:S(2)}, u32[]{:S(2)}) collective-permute-start(bf16[48,1920]{1,0:T(8,128)(2,1)S(1)} %get-tuple-element.32.refs_1_), channel_id=1, source_target_pairs={{0,1},{1,0},{2,3},{3,2},{4,5},{5,4},{6,7},{7,6},{8,9},{9,8},{10,11... | collective-permute-start | bytes 552968 | tf_op jit(solution)/shard_map/ppermute | solution.py:153
  18.0 6.1 %collective-permute-start.5 = (bf16[2,48,896]{2,1,0:T(8,128)(2,1)S(1)}, bf16[2,48,896]{2,1,0:T(8,128)(2,1)S(1)}, u32[]{:S(2)}, u32[]{:S(2)}) collective-permute-start(bf16[2,48,896]{2,1,0:T(8,128)(2,1)S(1)} %shard_map.125._), channel_id=1, source_target_pairs={{0,16},{1,9},{2,18},{3,11},{4,20},{5,13},{6,22},{7,15},{8,24},{9,1... | collective-permute-start | bytes 516104 | tf_op jit(solution)/shard_map/ppermute | solution.py:169
  21.7 2.4 %collective-permute-start.8 = (bf16[2,48,896]{2,1,0:T(8,128)(2,1)S(1)}, bf16[2,48,896]{2,1,0:T(8,128)(2,1)S(1)}, u32[]{:S(2)}, u32[]{:S(2)}) collective-permute-start(bf16[2,48,896]{2,1,0:T(8,128)(2,1)S(1)} %shard_map.127), channel_id=1, source_target_pairs={{0,1},{1,0},{2,3},{3,2},{4,5},{5,4},{6,7},{7,6},{8,9},{9,8},{10,11... | collective-permute-start | bytes 516104 | tf_op jit(solution)/shard_map/ppermute | solution.py:153
  22.3 1.8 %collective-permute-start.11 = (bf16[1,48,896]{2,1,0:T(8,128)(2,1)S(1)}, bf16[1,48,896]{2,1,0:T(8,128)(2,1)S(1)}, u32[]{:S(2)}, u32[]{:S(2)}) collective-permute-start(bf16[1,48,896]{2,1,0:T(8,128)(2,1)S(1)} %shard_map.128), channel_id=1, source_target_pairs={{0,1},{1,0},{2,3},{3,2},{4,5},{5,4},{6,7},{7,6},{8,9},{9,8},{10,11... | collective-permute-start | bytes 258056 | tf_op jit(solution)/shard_map/ppermute | solution.py:153
  24.1 2.4 %collective-permute-start.12 = (bf16[3,48,896]{2,1,0:T(8,128)(2,1)S(1)}, bf16[3,48,896]{2,1,0:T(8,128)(2,1)S(1)}, u32[]{:S(2)}, u32[]{:S(2)}) collective-permute-start(bf16[3,48,896]{2,1,0:T(8,128)(2,1)S(1)} %shard_map.129.refs_2_), channel_id=1, source_target_pairs={{0,1},{1,0},{2,3},{3,2},{4,5},{5,4},{6,7},{7,6},{8,9},{9,8},{10,11... | collective-permute-start | bytes 774152 | tf_op jit(solution)/shard_map/ppermute | solution.py:153
  26.0 2.4 %collective-permute-start.16 = (bf16[4,64,896]{2,1,0:T(8,128)(2,1)S(1)}, bf16[4,64,896]{2,1,0:T(8,128)(2,1)S(1)}, u32[]{:S(2)}, u32[]{:S(2)}) collective-permute-start(bf16[4,64,896]{2,1,0:T(8,128)(2,1)S(1)} %get-tuple-element.48), channel_id=1, source_target_pairs={{0,1},{1,0},{2,3},{3,2},{4,5},{5,4},{6,7},{7,6},{8,9},{9,8},{10,11... | collective-permute-start | bytes 1376264 | tf_op jit(solution)/shard_map/ppermute | solution.py:153
  28.3 1.9 %collective-permute-start.13 = (bf16[4,64,896]{2,1,0:T(8,128)(2,1)S(1)}, bf16[4,64,896]{2,1,0:T(8,128)(2,1)S(1)}, u32[]{:S(2)}, u32[]{:S(2)}) collective-permute-start(bf16[4,64,896]{2,1,0:T(8,128)(2,1)S(1)} %get-tuple-element.44), channel_id=1, source_target_pairs={{0,1},{1,0},{2,3},{3,2},{4,5},{5,4},{6,7},{7,6},{8,9},{9,8},{10,11... | collective-permute-start | bytes 1376264 | tf_op jit(solution)/shard_map/ppermute | solution.py:153
  28.5 4.9 %collective-permute-start.17 = (bf16[1,64,896]{2,1,0:T(8,128)(2,1)S(1)}, bf16[1,64,896]{2,1,0:T(8,128)(2,1)S(1)}, u32[]{:S(2)}, u32[]{:S(2)}) collective-permute-start(bf16[1,64,896]{2,1,0:T(8,128)(2,1)S(1)} %get-tuple-element.51), channel_id=1, source_target_pairs={{0,16},{1,9},{2,18},{3,11},{4,20},{5,13},{6,22},{7,15},{8,24},{9,1... | collective-permute-start | bytes 344072 | tf_op jit(solution)/shard_map/ppermute | solution.py:169
  30.3 4.9 %collective-permute-start.14 = (bf16[1,64,896]{2,1,0:T(8,128)(2,1)S(1)}, bf16[1,64,896]{2,1,0:T(8,128)(2,1)S(1)}, u32[]{:S(2)}, u32[]{:S(2)}) collective-permute-start(bf16[1,64,896]{2,1,0:T(8,128)(2,1)S(1)} %get-tuple-element.47._), channel_id=1, source_target_pairs={{0,16},{1,9},{2,18},{3,11},{4,20},{5,13},{6,22},{7,15},{8,24},{9,1... | collective-permute-start | bytes 344072 | tf_op jit(solution)/shard_map/ppermute | solution.py:169
  31.5 8.6 %collective-permute-start.19 = (bf16[2,64,896]{2,1,0:T(8,128)(2,1)S(1)}, bf16[2,64,896]{2,1,0:T(8,128)(2,1)S(1)}, u32[]{:S(2)}, u32[]{:S(2)}) collective-permute-start(bf16[2,64,896]{2,1,0:T(8,128)(2,1)S(1)} %shard_map.136), channel_id=1, source_target_pairs={{0,16},{1,9},{2,18},{3,11},{4,20},{5,13},{6,22},{7,15},{8,24},{9,1... | collective-permute-start | bytes 688136 | tf_op jit(solution)/shard_map/ppermute | solution.py:169
  33.4 4.9 %collective-permute-start.18 = (bf16[1,64,896]{2,1,0:T(8,128)(2,1)S(1)}, bf16[1,64,896]{2,1,0:T(8,128)(2,1)S(1)}, u32[]{:S(2)}, u32[]{:S(2)}) collective-permute-start(bf16[1,64,896]{2,1,0:T(8,128)(2,1)S(1)} %shard_map.135), channel_id=1, source_target_pairs={{0,8},{1,17},{2,10},{3,19},{4,12},{5,21},{6,14},{7,23},{8,0},{9,25... | collective-permute-start | bytes 344072 | tf_op jit(solution)/shard_map/ppermute | solution.py:169
  35.2 4.9 %collective-permute-start.15 = (bf16[1,64,896]{2,1,0:T(8,128)(2,1)S(1)}, bf16[1,64,896]{2,1,0:T(8,128)(2,1)S(1)}, u32[]{:S(2)}, u32[]{:S(2)}) collective-permute-start(bf16[1,64,896]{2,1,0:T(8,128)(2,1)S(1)} %shard_map.133), channel_id=1, source_target_pairs={{0,8},{1,17},{2,10},{3,19},{4,12},{5,21},{6,14},{7,23},{8,0},{9,25... | collective-permute-start | bytes 344072 | tf_op jit(solution)/shard_map/ppermute | solution.py:169
  40.2 6.5 %collective-permute-start.20 = (bf16[2,16,896]{2,1,0:T(8,128)(2,1)S(1)}, bf16[2,16,896]{2,1,0:T(8,128)(2,1)S(1)}, u32[]{:S(2)}, u32[]{:S(2)}) collective-permute-start(bf16[2,16,896]{2,1,0:T(8,128)(2,1)S(1)} %get-tuple-element.53), channel_id=1, source_target_pairs={{0,6},{1,7},{2,4},{3,5},{4,2},{5,3},{6,0},{7,1},{8,14},{9,15},{10,... | collective-permute-start | bytes 172040 | tf_op jit(solution)/shard_map/ppermute | solution.py:153
  42.5 6.1 %collective-permute-start.21 = (bf16[2,16,896]{2,1,0:T(8,128)(2,1)S(1)}, bf16[2,16,896]{2,1,0:T(8,128)(2,1)S(1)}, u32[]{:S(2)}, u32[]{:S(2)}) collective-permute-start(bf16[2,16,896]{2,1,0:T(8,128)(2,1)S(1)} %get-tuple-element.54), channel_id=1, source_target_pairs={{0,4},{1,5},{2,6},{3,7},{4,0},{5,1},{6,2},{7,3},{8,12},{9,13},{10,... | collective-permute-start | bytes 172040 | tf_op jit(solution)/shard_map/ppermute | solution.py:153
  42.8 5.8 %collective-permute-start.22 = (bf16[2,16,896]{2,1,0:T(8,128)(2,1)S(1)}, bf16[2,16,896]{2,1,0:T(8,128)(2,1)S(1)}, u32[]{:S(2)}, u32[]{:S(2)}) collective-permute-start(bf16[2,16,896]{2,1,0:T(8,128)(2,1)S(1)} %get-tuple-element.55), channel_id=1, source_target_pairs={{0,2},{1,3},{2,0},{3,1},{4,6},{5,7},{6,4},{7,5},{8,10},{9,11},{10,... | collective-permute-start | bytes 172040 | tf_op jit(solution)/shard_map/ppermute | solution.py:153
where the time goes:
time: 49.4 us; the launch traced here: 49.2 us
  starting transfers between devices  23.2 us (47%)
  waiting for transfers between devices  13.4 us (27%)
  Pallas kernels  11.9 us (24%)
  between operations  0.78 us (2%)
    pallas_call x17, Pallas kernels, call(): pl.pallas_call(kernel, out_shape=shapes, in_specs=[pl.BlockSpec(memory_sp...  11.9 us
    ppermute x13, starting transfers between devices, swap_expert(): return lax.ppermute(x, 'expert', [(i, i ^ mask) for i in range(size)])  11.2 us
    ppermute x7, starting transfers between devices, swap_halves(): return lax.ppermute(x, ('section', 'expert'), pairs)  8.48 us
    ppermute x7, waiting for transfers between devices, swap_halves(): return lax.ppermute(x, ('section', 'expert'), pairs)  7.07 us
    ppermute x13, waiting for transfers between devices, swap_expert(): return lax.ppermute(x, 'expert', [(i, i ^ mask) for i in range(size)])  5.92 us
    ppermute x3, starting transfers between devices, swap_section(): return lax.ppermute(x, 'section', [(i, i ^ mask) for i in range(size)])  3.49 us
  transfers between devices with their start and end apart: 23, of which 11 were waited for; matrix products, arithmetic and copies ran while one was open for 0% of the time, Pallas kernels for 20%

commit v1 on v0

--- a/solution.py
+++ b/solution.py
@@ -307,7 +307,7 @@
 
 
 def sent_order(sections):
-    return [sections - 1, *range(1, sections - 1)]
+    return [*range(1, sections - 2), sections - 1, sections - 2]
 
 
 def scale_column(m, experts, table_ref):

time: 49.4 us -> 49.5 us (level)
  starting transfers between devices: 23.2 us -> 24.9 us
  waiting for transfers between devices: 13.4 us -> 11.8 us
    ppermute x7, waiting for transfers between devices: 7.07 us -> 5.77 us  [swap_halves(): return lax.ppermute(x, ('section', 'expert'), pairs)]
    ppermute x7, starting transfers between devices: 8.48 us -> 9.42 us  [swap_halves(): return lax.ppermute(x, ('section', 'expert'), pairs)]
    ppermute x13, starting transfers between devices: 11.2 us -> 12 us  [swap_expert(): return lax.ppermute(x, 'expert', [(i, i ^ mask) for i in range(size)])]
  transfers between devices with their start and end apart: 23 -> 23, of which waited for: 11 -> 10; matrix products, arithmetic and copies ran while one was open for 0% -> 0% of each run, Pallas kernels for 20% -> 20%
where the time goes in v1:
time: 49.5 us; the launch traced here: 49.3 us
  starting transfers between devices  24.9 us (50%)
  Pallas kernels  11.9 us (24%)
  waiting for transfers between devices  11.8 us (24%)
  between operations  0.79 us (2%)
    ppermute x13, starting transfers between devices, swap_expert(): return lax.ppermute(x, 'expert', [(i, i ^ mask) for i in range(size)])  12 us
    pallas_call x17, Pallas kernels, call(): pl.pallas_call(kernel, out_shape=shapes, in_specs=[pl.BlockSpec(memory_sp...  11.9 us
    ppermute x7, starting transfers between devices, swap_halves(): return lax.ppermute(x, ('section', 'expert'), pairs)  9.42 us
    ppermute x13, waiting for transfers between devices, swap_expert(): return lax.ppermute(x, 'expert', [(i, i ^ mask) for i in range(size)])  5.99 us
    ppermute x7, waiting for transfers between devices, swap_halves(): return lax.ppermute(x, ('section', 'expert'), pairs)  5.77 us
    ppermute x3, starting transfers between devices, swap_section(): return lax.ppermute(x, 'section', [(i, i ^ mask) for i in range(size)])  3.49 us
  transfers between devices with their start and end apart: 23, of which 10 were waited for; matrix products, arithmetic and copies ran while one was open for 0% of the time, Pallas kernels for 20%

profile of v1, /device:TPU:0, one launch (start us, length us, event | category | flops | bytes accessed | tf_op | source)
XLA Modules:
  0.0 49.3 jit_solution(10765811820024208986)
XLA Ops:
  0.6 1.1 %shard_map.122 = (bf16[16,7296]{1,0:T(8,128)(2,1)S(1)}, bf16[16,1920]{1,0:T(8,128)(2,1)S(1)}) custom-call(bf16[16,3584]{1,0:T(8,128)(2,1)} %xa.1, s32[8,16]{1,0:T(8,128)} %bitcast.14, f32[8,16]{1,0:T(8,128)} %bitcast.15, bf16[16,3584]{1,0:T(8,128)(2,1)} %xb.1, s32[8,16]{1,0:T(8,128)} %bitcast.16, f32[8,16]{1,0:T(8,128)} %bitcast.17), custom_call_target="tpu_custom_call" | custom-call | tf_op jit(solution)/shard_map/pallas_call | solution.py:116
  1.7 0.5 %collective-permute-start.3 = (bf16[16,7296]{1,0:T(8,128)(2,1)S(1)}, bf16[16,7296]{1,0:T(8,128)(2,1)S(1)}, u32[]{:S(2)}, u32[]{:S(2)}) collective-permute-start(bf16[16,7296]{1,0:T(8,128)(2,1)S(1)} %get-tuple-element.29.refs_0_), channel_id=1, source_target_pairs={{0,1},{1,0},{2,3},{3,2},{4,5},{5,4},{6,7},{7,6},{8,9},{9,8},{10,11... | collective-permute-start | bytes 700424 | tf_op jit(solution)/shard_map/ppermute | solution.py:153
  2.2 4.7 %collective-permute-start.2 = (bf16[16,1920]{1,0:T(8,128)(2,1)S(1)}, bf16[16,1920]{1,0:T(8,128)(2,1)S(1)}, u32[]{:S(2)}, u32[]{:S(2)}) collective-permute-start(bf16[16,1920]{1,0:T(8,128)(2,1)S(1)} %get-tuple-element.30._), channel_id=1, source_target_pairs={{0,6},{1,7},{2,4},{3,5},{4,2},{5,3},{6,0},{7,1},{8,14},{9,15},{10,... | collective-permute-start | bytes 184328 | tf_op jit(solution)/shard_map/ppermute | solution.py:153
  6.9 0.6 %collective-permute-start = (bf16[16,1920]{1,0:T(8,128)(2,1)S(1)}, bf16[16,1920]{1,0:T(8,128)(2,1)S(1)}, u32[]{:S(2)}, u32[]{:S(2)}) collective-permute-start(bf16[16,1920]{1,0:T(8,128)(2,1)S(1)} %get-tuple-element.30._), channel_id=1, source_target_pairs={{0,2},{1,3},{2,0},{3,1},{4,6},{5,7},{6,4},{7,5},{8,10},{9,11},{10,... | collective-permute-start | bytes 184328 | tf_op jit(solution)/shard_map/ppermute | solution.py:153
  7.5 3.7 %shard_map.123 = (bf16[512,3584]{1,0:T(8,128)(2,1)S(1)}, bf16[3584,512]{1,0:T(8,128)(2,1)S(1)}, bf16[3584,512]{1,0:T(8,128)(2,1)S(1)}, bf16[512,3584]{1,0:T(8,12...) custom-call(bf16[512,3584]{1,0:T(8,128)(2,1)} %bitcast.9, bf16[3584,512]{1,0:T(8,128)(2,1)} %bitcast.10, ...), custom_call_target="tpu_custom_call" | custom-call | flops 1409286144 | bytes 11010048 | tf_op jit(solution)/shard_map/pallas_call | solution.py:116
  11.3 1.3 %collective-permute-done.1.refs_1_ = bf16[16,1920]{1,0:T(8,128)(2,1)S(1)} collective-permute-done((bf16[16,1920]{1,0:T(8,128)(2,1)S(1)}, bf16[16,1920]{1,0:T(8,128)(2,1)S(1)}, u32[]{:S(2)}, u32[]{:S(2)}) %collective-permute-start.1) | collective-permute-done | bytes 61472 | tf_op jit(solution)/shard_map/ppermute | solution.py:153
  12.7 1.6 %collective-permute-start.4 = (bf16[48,896]{1,0:T(8,128)(2,1)S(1)}, bf16[48,896]{1,0:T(8,128)(2,1)S(1)}, u32[]{:S(2)}, u32[]{:S(2)}) collective-permute-start(bf16[48,896]{1,0:T(8,128)(2,1)S(1)} %get-tuple-element.33.refs_0_), channel_id=1, source_target_pairs={{0,8},{1,17},{2,10},{3,19},{4,12},{5,21},{6,14},{7,23},{8,0},{9,25... | collective-permute-start | bytes 258056 | tf_op jit(solution)/shard_map/ppermute | solution.py:169
  14.2 1.5 %collective-permute-start.7 = (bf16[48,896]{1,0:T(8,128)(2,1)S(1)}, bf16[48,896]{1,0:T(8,128)(2,1)S(1)}, u32[]{:S(2)}, u32[]{:S(2)}) collective-permute-start(bf16[48,896]{1,0:T(8,128)(2,1)S(1)} %get-tuple-element.34), channel_id=1, source_target_pairs={{0,24},{8,16},{16,8},{24,0},{1,25},{9,17},{17,9},{25,1},{2,26},{10... | collective-permute-start | bytes 258056 | tf_op jit(solution)/shard_map/ppermute | solution.py:158
  15.7 1.5 %collective-permute-start.6 = (bf16[48,896]{1,0:T(8,128)(2,1)S(1)}, bf16[48,896]{1,0:T(8,128)(2,1)S(1)}, u32[]{:S(2)}, u32[]{:S(2)}) collective-permute-start(bf16[48,896]{1,0:T(8,128)(2,1)S(1)} %get-tuple-element.34), channel_id=1, source_target_pairs={{0,8},{8,0},{16,24},{24,16},{1,9},{9,1},{17,25},{25,17},{2,10},{10... | collective-permute-start | bytes 258056 | tf_op jit(solution)/shard_map/ppermute | solution.py:158
  17.2 0.5 %collective-permute-start.9 = (bf16[48,896]{1,0:T(8,128)(2,1)S(1)}, bf16[48,896]{1,0:T(8,128)(2,1)S(1)}, u32[]{:S(2)}, u32[]{:S(2)}) collective-permute-start(bf16[48,896]{1,0:T(8,128)(2,1)S(1)} %get-tuple-element.34), channel_id=1, source_target_pairs={{0,16},{8,24},{16,0},{24,8},{1,17},{9,25},{17,1},{25,9},{2,18},{10... | collective-permute-start | bytes 258056 | tf_op jit(solution)/shard_map/ppermute | solution.py:158
  17.7 0.3 collective-permute-done.4.refs_1_.refs_0_
  18.0 1.6 %collective-permute-start.5 = (bf16[2,48,896]{2,1,0:T(8,128)(2,1)S(1)}, bf16[2,48,896]{2,1,0:T(8,128)(2,1)S(1)}, u32[]{:S(2)}, u32[]{:S(2)}) collective-permute-start(bf16[2,48,896]{2,1,0:T(8,128)(2,1)S(1)} %shard_map.125._), channel_id=1, source_target_pairs={{0,16},{1,9},{2,18},{3,11},{4,20},{5,13},{6,22},{7,15},{8,24},{9,1... | collective-permute-start | bytes 516104 | tf_op jit(solution)/shard_map/ppermute | solution.py:169
  19.6 2.4 %shard_map.126 = (bf16[3584,512]{1,0:T(8,128)(2,1)S(1)}, bf16[512,3584]{1,0:T(8,128)(2,1)S(1)}) custom-call(bf16[3584,512]{1,0:T(8,128)(2,1)} %bitcast.11, bf16[2,48,896]{2,1,0:T(8,128)(2,1)S(1)} %shard_map.125._), custom_call_target="tpu_custom_call" | custom-call | flops 1000 | bytes 1000 | tf_op jit(solution)/shard_map/pallas_call | solution.py:116
  22.2 0.5 %collective-permute-start.11 = (bf16[1,48,896]{2,1,0:T(8,128)(2,1)S(1)}, bf16[1,48,896]{2,1,0:T(8,128)(2,1)S(1)}, u32[]{:S(2)}, u32[]{:S(2)}) collective-permute-start(bf16[1,48,896]{2,1,0:T(8,128)(2,1)S(1)} %shard_map.128), channel_id=1, source_target_pairs={{0,1},{1,0},{2,3},{3,2},{4,5},{5,4},{6,7},{7,6},{8,9},{9,8},{10,11... | collective-permute-start | bytes 258056 | tf_op jit(solution)/shard_map/ppermute | solution.py:153
  22.7 0.8 %collective-permute-done.5.refs_1_ = bf16[2,48,896]{2,1,0:T(8,128)(2,1)S(1)} collective-permute-done((bf16[2,48,896]{2,1,0:T(8,128)(2,1)S(1)}, bf16[2,48,896]{2,1,0:T(8,128)(2,1)S(1)}, u32[]{:S(2)}, u32[]{:S(2)}) %collective-permute-start.5) | collective-permute-done | bytes 172064 | tf_op jit(solution)/shard_map/ppermute | solution.py:169
  23.7 0.4 collective-permute-start.12
  24.1 1.8 %shard_map.130 = (bf16[4,64,896]{2,1,0:T(8,128)(2,1)S(1)}, bf16[4,64,896]{2,1,0:T(8,128)(2,1)S(1)}) custom-call(bf16[16,7296]{1,0:T(8,128)(2,1)S(1)} %get-tuple-element.29.refs_0_, bf16[48,1920]{1,0:T(8,128)(2,1)S(1)} %get-tuple-element.32.refs_1_, bf16[48,896]{1,0:T(8,128)(2,1)S(1)} %collective-permute-done.6.refs_0_.refs_2_, ...), custom_call_target="tpu_custom_call" | custom-call | flops 1000 | bytes 1000 | tf_op jit(solution)/shard_map/pallas_call | solution.py:116
  26.1 1.8 %shard_map.131 = (bf16[4,64,896]{2,1,0:T(8,128)(2,1)S(1)}, bf16[4,64,896]{2,1,0:T(8,128)(2,1)S(1)}) custom-call(bf16[16,7296]{1,0:T(8,128)(2,1)S(1)} %get-tuple-element.29.refs_0_, bf16[48,1920]{1,0:T(8,128)(2,1)S(1)} %get-tuple-element.32.refs_1_, bf16[3,48,896]{2,1,0:T(8,128)(2,1)S(1)} %shard_map.129.refs_2_, ...), custom_call_target="tpu_custom_call" | custom-call | flops 1000 | bytes 1000 | tf_op jit(solution)/shard_map/pallas_call | solution.py:116
  27.9 0.4 collective-permute-start.13
  28.4 1.1 %collective-permute-start.17 = (bf16[1,64,896]{2,1,0:T(8,128)(2,1)S(1)}, bf16[1,64,896]{2,1,0:T(8,128)(2,1)S(1)}, u32[]{:S(2)}, u32[]{:S(2)}) collective-permute-start(bf16[1,64,896]{2,1,0:T(8,128)(2,1)S(1)} %get-tuple-element.51), channel_id=1, source_target_pairs={{0,16},{1,9},{2,18},{3,11},{4,20},{5,13},{6,22},{7,15},{8,24},{9,1... | collective-permute-start | bytes 344072 | tf_op jit(solution)/shard_map/ppermute | solution.py:169
  29.9 1.5 %collective-permute-start.14 = (bf16[1,64,896]{2,1,0:T(8,128)(2,1)S(1)}, bf16[1,64,896]{2,1,0:T(8,128)(2,1)S(1)}, u32[]{:S(2)}, u32[]{:S(2)}) collective-permute-start(bf16[1,64,896]{2,1,0:T(8,128)(2,1)S(1)} %get-tuple-element.47._), channel_id=1, source_target_pairs={{0,16},{1,9},{2,18},{3,11},{4,20},{5,13},{6,22},{7,15},{8,24},{9,1... | collective-permute-start | bytes 344072 | tf_op jit(solution)/shard_map/ppermute | solution.py:169
  31.4 0.7 %collective-permute-start.19 = (bf16[2,64,896]{2,1,0:T(8,128)(2,1)S(1)}, bf16[2,64,896]{2,1,0:T(8,128)(2,1)S(1)}, u32[]{:S(2)}, u32[]{:S(2)}) collective-permute-start(bf16[2,64,896]{2,1,0:T(8,128)(2,1)S(1)} %shard_map.136), channel_id=1, source_target_pairs={{0,16},{1,9},{2,18},{3,11},{4,20},{5,13},{6,22},{7,15},{8,24},{9,1... | collective-permute-start | bytes 688136 | tf_op jit(solution)/shard_map/ppermute | solution.py:169
  32.1 1.2 %collective-permute-done.17.refs_1_ = bf16[1,64,896]{2,1,0:T(8,128)(2,1)S(1)} collective-permute-done((bf16[1,64,896]{2,1,0:T(8,128)(2,1)S(1)}, bf16[1,64,896]{2,1,0:T(8,128)(2,1)S(1)}, u32[]{:S(2)}, u32[]{:S(2)}) %collective-permute-start.17) | collective-permute-done | bytes 114720 | tf_op jit(solution)/shard_map/ppermute | solution.py:169
  33.3 1.6 %collective-permute-start.18 = (bf16[1,64,896]{2,1,0:T(8,128)(2,1)S(1)}, bf16[1,64,896]{2,1,0:T(8,128)(2,1)S(1)}, u32[]{:S(2)}, u32[]{:S(2)}) collective-permute-start(bf16[1,64,896]{2,1,0:T(8,128)(2,1)S(1)} %shard_map.135), channel_id=1, source_target_pairs={{0,8},{1,17},{2,10},{3,19},{4,12},{5,21},{6,14},{7,23},{8,0},{9,25... | collective-permute-start | bytes 344072 | tf_op jit(solution)/shard_map/ppermute | solution.py:169
  34.9 1.4 %collective-permute-start.15 = (bf16[1,64,896]{2,1,0:T(8,128)(2,1)S(1)}, bf16[1,64,896]{2,1,0:T(8,128)(2,1)S(1)}, u32[]{:S(2)}, u32[]{:S(2)}) collective-permute-start(bf16[1,64,896]{2,1,0:T(8,128)(2,1)S(1)} %shard_map.133), channel_id=1, source_target_pairs={{0,8},{1,17},{2,10},{3,19},{4,12},{5,21},{6,14},{7,23},{8,0},{9,25... | collective-permute-start | bytes 344072 | tf_op jit(solution)/shard_map/ppermute | solution.py:169
  36.3 1.8 %collective-permute-done.18.refs_3_ = bf16[1,64,896]{2,1,0:T(8,128)(2,1)S(1)} collective-permute-done((bf16[1,64,896]{2,1,0:T(8,128)(2,1)S(1)}, bf16[1,64,896]{2,1,0:T(8,128)(2,1)S(1)}, u32[]{:S(2)}, u32[]{:S(2)}) %collective-permute-start.18) | collective-permute-done | bytes 114720 | tf_op jit(solution)/shard_map/ppermute | solution.py:169
  38.2 1.6 %collective-permute-done.15.refs_1_ = bf16[1,64,896]{2,1,0:T(8,128)(2,1)S(1)} collective-permute-done((bf16[1,64,896]{2,1,0:T(8,128)(2,1)S(1)}, bf16[1,64,896]{2,1,0:T(8,128)(2,1)S(1)}, u32[]{:S(2)}, u32[]{:S(2)}) %collective-permute-start.15) | collective-permute-done | bytes 114720 | tf_op jit(solution)/shard_map/ppermute | solution.py:169
  39.8 2.6 %collective-permute-start.20 = (bf16[2,16,896]{2,1,0:T(8,128)(2,1)S(1)}, bf16[2,16,896]{2,1,0:T(8,128)(2,1)S(1)}, u32[]{:S(2)}, u32[]{:S(2)}) collective-permute-start(bf16[2,16,896]{2,1,0:T(8,128)(2,1)S(1)} %get-tuple-element.53), channel_id=1, source_target_pairs={{0,6},{1,7},{2,4},{3,5},{4,2},{5,3},{6,0},{7,1},{8,14},{9,15},{10,... | collective-permute-start | bytes 172040 | tf_op jit(solution)/shard_map/ppermute | solution.py:153
  42.8 1.5 %collective-permute-start.22 = (bf16[2,16,896]{2,1,0:T(8,128)(2,1)S(1)}, bf16[2,16,896]{2,1,0:T(8,128)(2,1)S(1)}, u32[]{:S(2)}, u32[]{:S(2)}) collective-permute-start(bf16[2,16,896]{2,1,0:T(8,128)(2,1)S(1)} %get-tuple-element.55), channel_id=1, source_target_pairs={{0,2},{1,3},{2,0},{3,1},{4,6},{5,7},{6,4},{7,5},{8,10},{9,11},{10,... | collective-permute-start | bytes 172040 | tf_op jit(solution)/shard_map/ppermute | solution.py:153
  44.3 2.1 %collective-permute-done.20.refs_1_ = bf16[2,16,896]{2,1,0:T(8,128)(2,1)S(1)} collective-permute-done((bf16[2,16,896]{2,1,0:T(8,128)(2,1)S(1)}, bf16[2,16,896]{2,1,0:T(8,128)(2,1)S(1)}, u32[]{:S(2)}, u32[]{:S(2)}) %collective-permute-start.20) | collective-permute-done | bytes 57376 | tf_op jit(solution)/shard_map/ppermute | solution.py:153
  46.4 2.3 %collective-permute-done.21.refs_2_ = bf16[2,16,896]{2,1,0:T(8,128)(2,1)S(1)} collective-permute-done((bf16[2,16,896]{2,1,0:T(8,128)(2,1)S(1)}, bf16[2,16,896]{2,1,0:T(8,128)(2,1)S(1)}, u32[]{:S(2)}, u32[]{:S(2)}) %collective-permute-start.21) | collective-permute-done | bytes 57376 | tf_op jit(solution)/shard_map/ppermute | solution.py:153
  48.6 0.6 %shard_map.138 = (bf16[16,896]{1,0:T(8,128)(2,1)}, bf16[16,896]{1,0:T(8,128)(2,1)}) custom-call(bf16[2,16,896]{2,1,0:T(8,128)(2,1)S(1)} %get-tuple-element.52.refs_0_, bf16[2,16,896]{2,1,0:T(8,128)(2,1)S(1)} %collective-permute-done.20.refs_1_, bf16[2,16,896]{2,1,0:T(8,128)(2,1)S(1)} %collective-permute-done.21.refs_2_, ...), custom_call_target="tpu_custom_call" | custom-call | tf_op jit(solution)/shard_map/pallas_call | solution.py:116
  (31 shorter events, 1.4 us)
Async XLA Ops:
  1.7 10.9 %collective-permute-start.3 = (bf16[16,7296]{1,0:T(8,128)(2,1)S(1)}, bf16[16,7296]{1,0:T(8,128)(2,1)S(1)}, u32[]{:S(2)}, u32[]{:S(2)}) collective-permute-start(bf16[16,7296]{1,0:T(8,128)(2,1)S(1)} %get-tuple-element.29.refs_0_), channel_id=1, source_target_pairs={{0,1},{1,0},{2,3},{3,2},{4,5},{5,4},{6,7},{7,6},{8,9},{9,8},{10,11... | collective-permute-start | bytes 700424 | tf_op jit(solution)/shard_map/ppermute | solution.py:153
  2.2 9.1 %collective-permute-start.2 = (bf16[16,1920]{1,0:T(8,128)(2,1)S(1)}, bf16[16,1920]{1,0:T(8,128)(2,1)S(1)}, u32[]{:S(2)}, u32[]{:S(2)}) collective-permute-start(bf16[16,1920]{1,0:T(8,128)(2,1)S(1)} %get-tuple-element.30._), channel_id=1, source_target_pairs={{0,6},{1,7},{2,4},{3,5},{4,2},{5,3},{6,0},{7,1},{8,14},{9,15},{10,... | collective-permute-start | bytes 184328 | tf_op jit(solution)/shard_map/ppermute | solution.py:153
  6.9 5.7 %collective-permute-start.1 = (bf16[16,1920]{1,0:T(8,128)(2,1)S(1)}, bf16[16,1920]{1,0:T(8,128)(2,1)S(1)}, u32[]{:S(2)}, u32[]{:S(2)}) collective-permute-start(bf16[16,1920]{1,0:T(8,128)(2,1)S(1)} %get-tuple-element.30._), channel_id=1, source_target_pairs={{0,4},{1,5},{2,6},{3,7},{4,0},{5,1},{6,2},{7,3},{8,12},{9,13},{10,... | collective-permute-start | bytes 184328 | tf_op jit(solution)/shard_map/ppermute | solution.py:153
  6.9 5.7 %collective-permute-start = (bf16[16,1920]{1,0:T(8,128)(2,1)S(1)}, bf16[16,1920]{1,0:T(8,128)(2,1)S(1)}, u32[]{:S(2)}, u32[]{:S(2)}) collective-permute-start(bf16[16,1920]{1,0:T(8,128)(2,1)S(1)} %get-tuple-element.30._), channel_id=1, source_target_pairs={{0,2},{1,3},{2,0},{3,1},{4,6},{5,7},{6,4},{7,5},{8,10},{9,11},{10,... | collective-permute-start | bytes 184328 | tf_op jit(solution)/shard_map/ppermute | solution.py:153
  12.7 5.4 %collective-permute-start.4 = (bf16[48,896]{1,0:T(8,128)(2,1)S(1)}, bf16[48,896]{1,0:T(8,128)(2,1)S(1)}, u32[]{:S(2)}, u32[]{:S(2)}) collective-permute-start(bf16[48,896]{1,0:T(8,128)(2,1)S(1)} %get-tuple-element.33.refs_0_), channel_id=1, source_target_pairs={{0,8},{1,17},{2,10},{3,19},{4,12},{5,21},{6,14},{7,23},{8,0},{9,25... | collective-permute-start | bytes 258056 | tf_op jit(solution)/shard_map/ppermute | solution.py:169
  14.2 7.8 %collective-permute-start.7 = (bf16[48,896]{1,0:T(8,128)(2,1)S(1)}, bf16[48,896]{1,0:T(8,128)(2,1)S(1)}, u32[]{:S(2)}, u32[]{:S(2)}) collective-permute-start(bf16[48,896]{1,0:T(8,128)(2,1)S(1)} %get-tuple-element.34), channel_id=1, source_target_pairs={{0,24},{8,16},{16,8},{24,0},{1,25},{9,17},{17,9},{25,1},{2,26},{10... | collective-permute-start | bytes 258056 | tf_op jit(solution)/shard_map/ppermute | solution.py:158
  15.7 6.3 %collective-permute-start.6 = (bf16[48,896]{1,0:T(8,128)(2,1)S(1)}, bf16[48,896]{1,0:T(8,128)(2,1)S(1)}, u32[]{:S(2)}, u32[]{:S(2)}) collective-permute-start(bf16[48,896]{1,0:T(8,128)(2,1)S(1)} %get-tuple-element.34), channel_id=1, source_target_pairs={{0,8},{8,0},{16,24},{24,16},{1,9},{9,1},{17,25},{25,17},{2,10},{10... | collective-permute-start | bytes 258056 | tf_op jit(solution)/shard_map/ppermute | solution.py:158
  17.2 4.9 %collective-permute-start.9 = (bf16[48,896]{1,0:T(8,128)(2,1)S(1)}, bf16[48,896]{1,0:T(8,128)(2,1)S(1)}, u32[]{:S(2)}, u32[]{:S(2)}) collective-permute-start(bf16[48,896]{1,0:T(8,128)(2,1)S(1)} %get-tuple-element.34), channel_id=1, source_target_pairs={{0,16},{8,24},{16,0},{24,8},{1,17},{9,25},{17,1},{25,9},{2,18},{10... | collective-permute-start | bytes 258056 | tf_op jit(solution)/shard_map/ppermute | solution.py:158
  17.7 4.4 %collective-permute-start.10 = (bf16[48,1920]{1,0:T(8,128)(2,1)S(1)}, bf16[48,1920]{1,0:T(8,128)(2,1)S(1)}, u32[]{:S(2)}, u32[]{:S(2)}) collective-permute-start(bf16[48,1920]{1,0:T(8,128)(2,1)S(1)} %get-tuple-element.32.refs_1_), channel_id=1, source_target_pairs={{0,1},{1,0},{2,3},{3,2},{4,5},{5,4},{6,7},{7,6},{8,9},{9,8},{10,11... | collective-permute-start | bytes 552968 | tf_op jit(solution)/shard_map/ppermute | solution.py:153
  18.0 5.5 %collective-permute-start.5 = (bf16[2,48,896]{2,1,0:T(8,128)(2,1)S(1)}, bf16[2,48,896]{2,1,0:T(8,128)(2,1)S(1)}, u32[]{:S(2)}, u32[]{:S(2)}) collective-permute-start(bf16[2,48,896]{2,1,0:T(8,128)(2,1)S(1)} %shard_map.125._), channel_id=1, source_target_pairs={{0,16},{1,9},{2,18},{3,11},{4,20},{5,13},{6,22},{7,15},{8,24},{9,1... | collective-permute-start | bytes 516104 | tf_op jit(solution)/shard_map/ppermute | solution.py:169
  22.1 1.5 %collective-permute-start.8 = (bf16[2,48,896]{2,1,0:T(8,128)(2,1)S(1)}, bf16[2,48,896]{2,1,0:T(8,128)(2,1)S(1)}, u32[]{:S(2)}, u32[]{:S(2)}) collective-permute-start(bf16[2,48,896]{2,1,0:T(8,128)(2,1)S(1)} %shard_map.127), channel_id=1, source_target_pairs={{0,1},{1,0},{2,3},{3,2},{4,5},{5,4},{6,7},{7,6},{8,9},{9,8},{10,11... | collective-permute-start | bytes 516104 | tf_op jit(solution)/shard_map/ppermute | solution.py:153
  22.2 1.5 %collective-permute-start.11 = (bf16[1,48,896]{2,1,0:T(8,128)(2,1)S(1)}, bf16[1,48,896]{2,1,0:T(8,128)(2,1)S(1)}, u32[]{:S(2)}, u32[]{:S(2)}) collective-permute-start(bf16[1,48,896]{2,1,0:T(8,128)(2,1)S(1)} %shard_map.128), channel_id=1, source_target_pairs={{0,1},{1,0},{2,3},{3,2},{4,5},{5,4},{6,7},{7,6},{8,9},{9,8},{10,11... | collective-permute-start | bytes 258056 | tf_op jit(solution)/shard_map/ppermute | solution.py:153
  23.7 2.4 %collective-permute-start.12 = (bf16[3,48,896]{2,1,0:T(8,128)(2,1)S(1)}, bf16[3,48,896]{2,1,0:T(8,128)(2,1)S(1)}, u32[]{:S(2)}, u32[]{:S(2)}) collective-permute-start(bf16[3,48,896]{2,1,0:T(8,128)(2,1)S(1)} %shard_map.129.refs_2_), channel_id=1, source_target_pairs={{0,1},{1,0},{2,3},{3,2},{4,5},{5,4},{6,7},{7,6},{8,9},{9,8},{10,11... | collective-permute-start | bytes 774152 | tf_op jit(solution)/shard_map/ppermute | solution.py:153
  25.9 2.4 %collective-permute-start.16 = (bf16[4,64,896]{2,1,0:T(8,128)(2,1)S(1)}, bf16[4,64,896]{2,1,0:T(8,128)(2,1)S(1)}, u32[]{:S(2)}, u32[]{:S(2)}) collective-permute-start(bf16[4,64,896]{2,1,0:T(8,128)(2,1)S(1)} %get-tuple-element.48), channel_id=1, source_target_pairs={{0,1},{1,0},{2,3},{3,2},{4,5},{5,4},{6,7},{7,6},{8,9},{9,8},{10,11... | collective-permute-start | bytes 1376264 | tf_op jit(solution)/shard_map/ppermute | solution.py:153
  27.9 1.9 %collective-permute-start.13 = (bf16[4,64,896]{2,1,0:T(8,128)(2,1)S(1)}, bf16[4,64,896]{2,1,0:T(8,128)(2,1)S(1)}, u32[]{:S(2)}, u32[]{:S(2)}) collective-permute-start(bf16[4,64,896]{2,1,0:T(8,128)(2,1)S(1)} %get-tuple-element.44), channel_id=1, source_target_pairs={{0,1},{1,0},{2,3},{3,2},{4,5},{5,4},{6,7},{7,6},{8,9},{9,8},{10,11... | collective-permute-start | bytes 1376264 | tf_op jit(solution)/shard_map/ppermute | solution.py:153
  28.4 4.9 %collective-permute-start.17 = (bf16[1,64,896]{2,1,0:T(8,128)(2,1)S(1)}, bf16[1,64,896]{2,1,0:T(8,128)(2,1)S(1)}, u32[]{:S(2)}, u32[]{:S(2)}) collective-permute-start(bf16[1,64,896]{2,1,0:T(8,128)(2,1)S(1)} %get-tuple-element.51), channel_id=1, source_target_pairs={{0,16},{1,9},{2,18},{3,11},{4,20},{5,13},{6,22},{7,15},{8,24},{9,1... | collective-permute-start | bytes 344072 | tf_op jit(solution)/shard_map/ppermute | solution.py:169
  29.9 5.0 %collective-permute-start.14 = (bf16[1,64,896]{2,1,0:T(8,128)(2,1)S(1)}, bf16[1,64,896]{2,1,0:T(8,128)(2,1)S(1)}, u32[]{:S(2)}, u32[]{:S(2)}) collective-permute-start(bf16[1,64,896]{2,1,0:T(8,128)(2,1)S(1)} %get-tuple-element.47._), channel_id=1, source_target_pairs={{0,16},{1,9},{2,18},{3,11},{4,20},{5,13},{6,22},{7,15},{8,24},{9,1... | collective-permute-start | bytes 344072 | tf_op jit(solution)/shard_map/ppermute | solution.py:169
  31.4 8.4 %collective-permute-start.19 = (bf16[2,64,896]{2,1,0:T(8,128)(2,1)S(1)}, bf16[2,64,896]{2,1,0:T(8,128)(2,1)S(1)}, u32[]{:S(2)}, u32[]{:S(2)}) collective-permute-start(bf16[2,64,896]{2,1,0:T(8,128)(2,1)S(1)} %shard_map.136), channel_id=1, source_target_pairs={{0,16},{1,9},{2,18},{3,11},{4,20},{5,13},{6,22},{7,15},{8,24},{9,1... | collective-permute-start | bytes 688136 | tf_op jit(solution)/shard_map/ppermute | solution.py:169
  33.3 4.9 %collective-permute-start.18 = (bf16[1,64,896]{2,1,0:T(8,128)(2,1)S(1)}, bf16[1,64,896]{2,1,0:T(8,128)(2,1)S(1)}, u32[]{:S(2)}, u32[]{:S(2)}) collective-permute-start(bf16[1,64,896]{2,1,0:T(8,128)(2,1)S(1)} %shard_map.135), channel_id=1, source_target_pairs={{0,8},{1,17},{2,10},{3,19},{4,12},{5,21},{6,14},{7,23},{8,0},{9,25... | collective-permute-start | bytes 344072 | tf_op jit(solution)/shard_map/ppermute | solution.py:169
  34.9 4.9 %collective-permute-start.15 = (bf16[1,64,896]{2,1,0:T(8,128)(2,1)S(1)}, bf16[1,64,896]{2,1,0:T(8,128)(2,1)S(1)}, u32[]{:S(2)}, u32[]{:S(2)}) collective-permute-start(bf16[1,64,896]{2,1,0:T(8,128)(2,1)S(1)} %shard_map.133), channel_id=1, source_target_pairs={{0,8},{1,17},{2,10},{3,19},{4,12},{5,21},{6,14},{7,23},{8,0},{9,25... | collective-permute-start | bytes 344072 | tf_op jit(solution)/shard_map/ppermute | solution.py:169
  39.8 6.5 %collective-permute-start.20 = (bf16[2,16,896]{2,1,0:T(8,128)(2,1)S(1)}, bf16[2,16,896]{2,1,0:T(8,128)(2,1)S(1)}, u32[]{:S(2)}, u32[]{:S(2)}) collective-permute-start(bf16[2,16,896]{2,1,0:T(8,128)(2,1)S(1)} %get-tuple-element.53), channel_id=1, source_target_pairs={{0,6},{1,7},{2,4},{3,5},{4,2},{5,3},{6,0},{7,1},{8,14},{9,15},{10,... | collective-permute-start | bytes 172040 | tf_op jit(solution)/shard_map/ppermute | solution.py:153
  42.5 6.1 %collective-permute-start.21 = (bf16[2,16,896]{2,1,0:T(8,128)(2,1)S(1)}, bf16[2,16,896]{2,1,0:T(8,128)(2,1)S(1)}, u32[]{:S(2)}, u32[]{:S(2)}) collective-permute-start(bf16[2,16,896]{2,1,0:T(8,128)(2,1)S(1)} %get-tuple-element.54), channel_id=1, source_target_pairs={{0,4},{1,5},{2,6},{3,7},{4,0},{5,1},{6,2},{7,3},{8,12},{9,13},{10,... | collective-permute-start | bytes 172040 | tf_op jit(solution)/shard_map/ppermute | solution.py:153
  42.8 5.8 %collective-permute-start.22 = (bf16[2,16,896]{2,1,0:T(8,128)(2,1)S(1)}, bf16[2,16,896]{2,1,0:T(8,128)(2,1)S(1)}, u32[]{:S(2)}, u32[]{:S(2)}) collective-permute-start(bf16[2,16,896]{2,1,0:T(8,128)(2,1)S(1)} %get-tuple-element.55), channel_id=1, source_target_pairs={{0,2},{1,3},{2,0},{3,1},{4,6},{5,7},{6,4},{7,5},{8,10},{9,11},{10,... | collective-permute-start | bytes 172040 | tf_op jit(solution)/shard_map/ppermute | solution.py:153

commit v2 on v0

--- a/solution.py
+++ b/solution.py
@@ -573,7 +573,7 @@
         partial[m] = parts
     high, near = {}, {}
     for m in ("b", "a"):
-        *near[m], high[m] = add(partial[m], [1, 1, None, 1], quick)
+        (high[m],) = add(partial[m], [None, None, None, 1], quick)
     low = call(
         low_sum_kernel,
         [((2, half, width), dtype)],
@@ -582,6 +582,8 @@
         after=[4],
     )[0]
     got_low = swap_halves(low, 1, steps)
+    for m in ("b", "a"):
+        near[m] = add(partial[m], [1, 1, None, None], quick, [low])
     held = {}
     for m in ("b", "a"):
         kept, away = near[m]

time: 49.4 us -> 49.4 us (level)
    pallas_call x17 -> x19, Pallas kernels: 11.9 us -> 11.9 us  [call(): pl.pallas_call(kernel, out_shape=shapes, in_specs=[pl.BlockSpec(memory_sp...]
where the time goes in v2:
time: 49.4 us; the launch traced here: 49.2 us
  starting transfers between devices  23.2 us (47%)
  waiting for transfers between devices  13.4 us (27%)
  Pallas kernels  11.9 us (24%)
  between operations  0.79 us (2%)
    pallas_call x19, Pallas kernels, call(): pl.pallas_call(kernel, out_shape=shapes, in_specs=[pl.BlockSpec(memory_sp...  11.9 us
    ppermute x13, starting transfers between devices, swap_expert(): return lax.ppermute(x, 'expert', [(i, i ^ mask) for i in range(size)])  11.2 us
    ppermute x7, starting transfers between devices, swap_halves(): return lax.ppermute(x, ('section', 'expert'), pairs)  8.48 us
    ppermute x7, waiting for transfers between devices, swap_halves(): return lax.ppermute(x, ('section', 'expert'), pairs)  6.95 us
    ppermute x13, waiting for transfers between devices, swap_expert(): return lax.ppermute(x, 'expert', [(i, i ^ mask) for i in range(size)])  5.98 us
    ppermute x3, starting transfers between devices, swap_section(): return lax.ppermute(x, 'section', [(i, i ^ mask) for i in range(size)])  3.49 us
  transfers between devices with their start and end apart: 23, of which 11 were waited for; matrix products, arithmetic and copies ran while one was open for 0% of the time, Pallas kernels for 20%

profile of v2, /device:TPU:0, one launch (start us, length us, event | category | flops | bytes accessed | tf_op | source)
XLA Modules:
  0.0 49.2 jit_solution(12359707920605546119)
XLA Ops:
  0.6 1.1 %shard_map.122 = (bf16[16,7296]{1,0:T(8,128)(2,1)S(1)}, bf16[16,1920]{1,0:T(8,128)(2,1)S(1)}) custom-call(bf16[16,3584]{1,0:T(8,128)(2,1)} %xa.1, s32[8,16]{1,0:T(8,128)} %bitcast.14, f32[8,16]{1,0:T(8,128)} %bitcast.15, bf16[16,3584]{1,0:T(8,128)(2,1)} %xb.1, s32[8,16]{1,0:T(8,128)} %bitcast.16, f32[8,16]{1,0:T(8,128)} %bitcast.17), custom_call_target="tpu_custom_call" | custom-call | tf_op jit(solution)/shard_map/pallas_call | solution.py:116
  1.7 0.5 %collective-permute-start.3 = (bf16[16,7296]{1,0:T(8,128)(2,1)S(1)}, bf16[16,7296]{1,0:T(8,128)(2,1)S(1)}, u32[]{:S(2)}, u32[]{:S(2)}) collective-permute-start(bf16[16,7296]{1,0:T(8,128)(2,1)S(1)} %get-tuple-element.27.refs_0_), channel_id=1, source_target_pairs={{0,1},{1,0},{2,3},{3,2},{4,5},{5,4},{6,7},{7,6},{8,9},{9,8},{10,11... | collective-permute-start | bytes 700424 | tf_op jit(solution)/shard_map/ppermute | solution.py:153
  2.2 4.7 %collective-permute-start.2 = (bf16[16,1920]{1,0:T(8,128)(2,1)S(1)}, bf16[16,1920]{1,0:T(8,128)(2,1)S(1)}, u32[]{:S(2)}, u32[]{:S(2)}) collective-permute-start(bf16[16,1920]{1,0:T(8,128)(2,1)S(1)} %get-tuple-element.28._), channel_id=1, source_target_pairs={{0,6},{1,7},{2,4},{3,5},{4,2},{5,3},{6,0},{7,1},{8,14},{9,15},{10,... | collective-permute-start | bytes 184328 | tf_op jit(solution)/shard_map/ppermute | solution.py:153
  6.9 0.6 %collective-permute-start = (bf16[16,1920]{1,0:T(8,128)(2,1)S(1)}, bf16[16,1920]{1,0:T(8,128)(2,1)S(1)}, u32[]{:S(2)}, u32[]{:S(2)}) collective-permute-start(bf16[16,1920]{1,0:T(8,128)(2,1)S(1)} %get-tuple-element.28._), channel_id=1, source_target_pairs={{0,2},{1,3},{2,0},{3,1},{4,6},{5,7},{6,4},{7,5},{8,10},{9,11},{10,... | collective-permute-start | bytes 184328 | tf_op jit(solution)/shard_map/ppermute | solution.py:153
  7.5 3.7 %shard_map.123 = (bf16[512,3584]{1,0:T(8,128)(2,1)S(1)}, bf16[3584,512]{1,0:T(8,128)(2,1)S(1)}, bf16[3584,512]{1,0:T(8,128)(2,1)S(1)}, bf16[512,3584]{1,0:T(8,12...) custom-call(bf16[512,3584]{1,0:T(8,128)(2,1)} %bitcast.9, bf16[3584,512]{1,0:T(8,128)(2,1)} %bitcast.10, ...), custom_call_target="tpu_custom_call" | custom-call | flops 1409286144 | bytes 11010048 | tf_op jit(solution)/shard_map/pallas_call | solution.py:116
  11.3 1.3 %collective-permute-done.1.refs_1_ = bf16[16,1920]{1,0:T(8,128)(2,1)S(1)} collective-permute-done((bf16[16,1920]{1,0:T(8,128)(2,1)S(1)}, bf16[16,1920]{1,0:T(8,128)(2,1)S(1)}, u32[]{:S(2)}, u32[]{:S(2)}) %collective-permute-start.1) | collective-permute-done | bytes 61472 | tf_op jit(solution)/shard_map/ppermute | solution.py:153
  12.7 1.6 %collective-permute-start.4 = (bf16[48,896]{1,0:T(8,128)(2,1)S(1)}, bf16[48,896]{1,0:T(8,128)(2,1)S(1)}, u32[]{:S(2)}, u32[]{:S(2)}) collective-permute-start(bf16[48,896]{1,0:T(8,128)(2,1)S(1)} %get-tuple-element.31.refs_0_), channel_id=1, source_target_pairs={{0,8},{1,17},{2,10},{3,19},{4,12},{5,21},{6,14},{7,23},{8,0},{9,25... | collective-permute-start | bytes 258056 | tf_op jit(solution)/shard_map/ppermute | solution.py:169
  14.2 0.5 %collective-permute-start.7 = (bf16[48,896]{1,0:T(8,128)(2,1)S(1)}, bf16[48,896]{1,0:T(8,128)(2,1)S(1)}, u32[]{:S(2)}, u32[]{:S(2)}) collective-permute-start(bf16[48,896]{1,0:T(8,128)(2,1)S(1)} %get-tuple-element.32), channel_id=1, source_target_pairs={{0,8},{8,0},{16,24},{24,16},{1,9},{9,1},{17,25},{25,17},{2,10},{10... | collective-permute-start | bytes 258056 | tf_op jit(solution)/shard_map/ppermute | solution.py:158
  14.8 2.4 %collective-permute-start.6 = (bf16[48,896]{1,0:T(8,128)(2,1)S(1)}, bf16[48,896]{1,0:T(8,128)(2,1)S(1)}, u32[]{:S(2)}, u32[]{:S(2)}) collective-permute-start(bf16[48,896]{1,0:T(8,128)(2,1)S(1)} %get-tuple-element.32), channel_id=1, source_target_pairs={{0,24},{8,16},{16,8},{24,0},{1,25},{9,17},{17,9},{25,1},{2,26},{10... | collective-permute-start | bytes 258056 | tf_op jit(solution)/shard_map/ppermute | solution.py:158
  17.2 0.5 %collective-permute-start.9 = (bf16[48,896]{1,0:T(8,128)(2,1)S(1)}, bf16[48,896]{1,0:T(8,128)(2,1)S(1)}, u32[]{:S(2)}, u32[]{:S(2)}) collective-permute-start(bf16[48,896]{1,0:T(8,128)(2,1)S(1)} %get-tuple-element.32), channel_id=1, source_target_pairs={{0,16},{8,24},{16,0},{24,8},{1,17},{9,25},{17,1},{25,9},{2,18},{10... | collective-permute-start | bytes 258056 | tf_op jit(solution)/shard_map/ppermute | solution.py:158
  18.0 1.3 %collective-permute-start.5 = (bf16[2,48,896]{2,1,0:T(8,128)(2,1)S(1)}, bf16[2,48,896]{2,1,0:T(8,128)(2,1)S(1)}, u32[]{:S(2)}, u32[]{:S(2)}) collective-permute-start(bf16[2,48,896]{2,1,0:T(8,128)(2,1)S(1)} %shard_map.125._), channel_id=1, source_target_pairs={{0,16},{1,9},{2,18},{3,11},{4,20},{5,13},{6,22},{7,15},{8,24},{9,1... | collective-permute-start | bytes 516104 | tf_op jit(solution)/shard_map/ppermute | solution.py:169
  19.3 2.4 %shard_map.126 = (bf16[3584,512]{1,0:T(8,128)(2,1)S(1)}, bf16[512,3584]{1,0:T(8,128)(2,1)S(1)}) custom-call(bf16[3584,512]{1,0:T(8,128)(2,1)} %bitcast.11, bf16[2,48,896]{2,1,0:T(8,128)(2,1)S(1)} %shard_map.125._), custom_call_target="tpu_custom_call" | custom-call | flops 1000 | bytes 1000 | tf_op jit(solution)/shard_map/pallas_call | solution.py:116
  21.8 0.4 collective-permute-done.9.refs_0_.refs_3_
  22.4 1.7 %collective-permute-done.5.refs_1_ = bf16[2,48,896]{2,1,0:T(8,128)(2,1)S(1)} collective-permute-done((bf16[2,48,896]{2,1,0:T(8,128)(2,1)S(1)}, bf16[2,48,896]{2,1,0:T(8,128)(2,1)S(1)}, u32[]{:S(2)}, u32[]{:S(2)}) %collective-permute-start.5) | collective-permute-done | bytes 172064 | tf_op jit(solution)/shard_map/ppermute | solution.py:169
  24.2 1.8 %shard_map.130 = (bf16[4,64,896]{2,1,0:T(8,128)(2,1)S(1)}, bf16[4,64,896]{2,1,0:T(8,128)(2,1)S(1)}) custom-call(bf16[16,7296]{1,0:T(8,128)(2,1)S(1)} %get-tuple-element.27.refs_0_, bf16[48,1920]{1,0:T(8,128)(2,1)S(1)} %get-tuple-element.30.refs_1_, bf16[48,896]{1,0:T(8,128)(2,1)S(1)} %collective-permute-done.7.refs_1_.refs_2_, ...), custom_call_target="tpu_custom_call" | custom-call | flops 1000 | bytes 1000 | tf_op jit(solution)/shard_map/pallas_call | solution.py:116
  26.0 0.6 %collective-permute-start.14 = (bf16[4,64,896]{2,1,0:T(8,128)(2,1)S(1)}, bf16[4,64,896]{2,1,0:T(8,128)(2,1)S(1)}, u32[]{:S(2)}, u32[]{:S(2)}) collective-permute-start(bf16[4,64,896]{2,1,0:T(8,128)(2,1)S(1)} %get-tuple-element.43), channel_id=1, source_target_pairs={{0,1},{1,0},{2,3},{3,2},{4,5},{5,4},{6,7},{7,6},{8,9},{9,8},{10,11... | collective-permute-start | bytes 1376264 | tf_op jit(solution)/shard_map/ppermute | solution.py:153
  26.6 1.8 %shard_map.131 = (bf16[4,64,896]{2,1,0:T(8,128)(2,1)S(1)}, bf16[4,64,896]{2,1,0:T(8,128)(2,1)S(1)}) custom-call(bf16[16,7296]{1,0:T(8,128)(2,1)S(1)} %get-tuple-element.27.refs_0_, bf16[48,1920]{1,0:T(8,128)(2,1)S(1)} %get-tuple-element.30.refs_1_, bf16[3,48,896]{2,1,0:T(8,128)(2,1)S(1)} %shard_map.129.refs_2_, ...), custom_call_target="tpu_custom_call" | custom-call | flops 1000 | bytes 1000 | tf_op jit(solution)/shard_map/pallas_call | solution.py:116
  28.5 1.1 %collective-permute-start.17 = (bf16[1,64,896]{2,1,0:T(8,128)(2,1)S(1)}, bf16[1,64,896]{2,1,0:T(8,128)(2,1)S(1)}, u32[]{:S(2)}, u32[]{:S(2)}) collective-permute-start(bf16[1,64,896]{2,1,0:T(8,128)(2,1)S(1)} %shard_map.137), channel_id=1, source_target_pairs={{0,16},{1,9},{2,18},{3,11},{4,20},{5,13},{6,22},{7,15},{8,24},{9,1... | collective-permute-start | bytes 344072 | tf_op jit(solution)/shard_map/ppermute | solution.py:169
  29.6 0.7 %collective-permute-done.13.refs_1_.got_a = bf16[4,64,896]{2,1,0:T(8,128)(2,1)S(1)} collective-permute-done((bf16[4,64,896]{2,1,0:T(8,128)(2,1)S(1)}, bf16[4,64,896]{2,1,0:T(8,128)(2,1)S(1)}, u32[]{:S(2)}, u32[]{:S(2)}) %collective-permute-start.13) | collective-permute-done | bytes 458784 | tf_op jit(solution)/shard_map/ppermute | solution.py:153
  30.3 1.1 %collective-permute-start.15 = (bf16[1,64,896]{2,1,0:T(8,128)(2,1)S(1)}, bf16[1,64,896]{2,1,0:T(8,128)(2,1)S(1)}, u32[]{:S(2)}, u32[]{:S(2)}) collective-permute-start(bf16[1,64,896]{2,1,0:T(8,128)(2,1)S(1)} %shard_map.132._), channel_id=1, source_target_pairs={{0,16},{1,9},{2,18},{3,11},{4,20},{5,13},{6,22},{7,15},{8,24},{9,1... | collective-permute-start | bytes 344072 | tf_op jit(solution)/shard_map/ppermute | solution.py:169
  31.4 1.1 %collective-permute-start.19 = (bf16[2,64,896]{2,1,0:T(8,128)(2,1)S(1)}, bf16[2,64,896]{2,1,0:T(8,128)(2,1)S(1)}, u32[]{:S(2)}, u32[]{:S(2)}) collective-permute-start(bf16[2,64,896]{2,1,0:T(8,128)(2,1)S(1)} %shard_map.133.refs_2_), channel_id=1, source_target_pairs={{0,16},{1,9},{2,18},{3,11},{4,20},{5,13},{6,22},{7,15},{8,24},{9,1... | collective-permute-start | bytes 688136 | tf_op jit(solution)/shard_map/ppermute | solution.py:169
  32.5 0.8 %collective-permute-done.17.refs_1_ = bf16[1,64,896]{2,1,0:T(8,128)(2,1)S(1)} collective-permute-done((bf16[1,64,896]{2,1,0:T(8,128)(2,1)S(1)}, bf16[1,64,896]{2,1,0:T(8,128)(2,1)S(1)}, u32[]{:S(2)}, u32[]{:S(2)}) %collective-permute-start.17) | collective-permute-done | bytes 114720 | tf_op jit(solution)/shard_map/ppermute | solution.py:169
  33.4 1.3 %collective-permute-start.18 = (bf16[1,64,896]{2,1,0:T(8,128)(2,1)S(1)}, bf16[1,64,896]{2,1,0:T(8,128)(2,1)S(1)}, u32[]{:S(2)}, u32[]{:S(2)}) collective-permute-start(bf16[1,64,896]{2,1,0:T(8,128)(2,1)S(1)} %shard_map.138), channel_id=1, source_target_pairs={{0,8},{1,17},{2,10},{3,19},{4,12},{5,21},{6,14},{7,23},{8,0},{9,25... | collective-permute-start | bytes 344072 | tf_op jit(solution)/shard_map/ppermute | solution.py:169
  34.8 0.4 collective-permute-done.15.refs_1_
  35.2 1.0 %collective-permute-start.16 = (bf16[1,64,896]{2,1,0:T(8,128)(2,1)S(1)}, bf16[1,64,896]{2,1,0:T(8,128)(2,1)S(1)}, u32[]{:S(2)}, u32[]{:S(2)}) collective-permute-start(bf16[1,64,896]{2,1,0:T(8,128)(2,1)S(1)} %shard_map.135), channel_id=1, source_target_pairs={{0,8},{1,17},{2,10},{3,19},{4,12},{5,21},{6,14},{7,23},{8,0},{9,25... | collective-permute-start | bytes 344072 | tf_op jit(solution)/shard_map/ppermute | solution.py:169
  36.2 2.1 %collective-permute-done.18.refs_3_ = bf16[1,64,896]{2,1,0:T(8,128)(2,1)S(1)} collective-permute-done((bf16[1,64,896]{2,1,0:T(8,128)(2,1)S(1)}, bf16[1,64,896]{2,1,0:T(8,128)(2,1)S(1)}, u32[]{:S(2)}, u32[]{:S(2)}) %collective-permute-start.18) | collective-permute-done | bytes 114720 | tf_op jit(solution)/shard_map/ppermute | solution.py:169
  38.2 1.8 %collective-permute-done.16.refs_1_ = bf16[1,64,896]{2,1,0:T(8,128)(2,1)S(1)} collective-permute-done((bf16[1,64,896]{2,1,0:T(8,128)(2,1)S(1)}, bf16[1,64,896]{2,1,0:T(8,128)(2,1)S(1)}, u32[]{:S(2)}, u32[]{:S(2)}) %collective-permute-start.16) | collective-permute-done | bytes 114720 | tf_op jit(solution)/shard_map/ppermute | solution.py:169
  40.1 2.4 %collective-permute-start.20 = (bf16[2,16,896]{2,1,0:T(8,128)(2,1)S(1)}, bf16[2,16,896]{2,1,0:T(8,128)(2,1)S(1)}, u32[]{:S(2)}, u32[]{:S(2)}) collective-permute-start(bf16[2,16,896]{2,1,0:T(8,128)(2,1)S(1)} %get-tuple-element.49), channel_id=1, source_target_pairs={{0,6},{1,7},{2,4},{3,5},{4,2},{5,3},{6,0},{7,1},{8,14},{9,15},{10,... | collective-permute-start | bytes 172040 | tf_op jit(solution)/shard_map/ppermute | solution.py:153
  42.7 1.9 %collective-permute-start.22 = (bf16[2,16,896]{2,1,0:T(8,128)(2,1)S(1)}, bf16[2,16,896]{2,1,0:T(8,128)(2,1)S(1)}, u32[]{:S(2)}, u32[]{:S(2)}) collective-permute-start(bf16[2,16,896]{2,1,0:T(8,128)(2,1)S(1)} %get-tuple-element.51), channel_id=1, source_target_pairs={{0,2},{1,3},{2,0},{3,1},{4,6},{5,7},{6,4},{7,5},{8,10},{9,11},{10,... | collective-permute-start | bytes 172040 | tf_op jit(solution)/shard_map/ppermute | solution.py:153
  44.6 2.1 %collective-permute-done.20.refs_1_ = bf16[2,16,896]{2,1,0:T(8,128)(2,1)S(1)} collective-permute-done((bf16[2,16,896]{2,1,0:T(8,128)(2,1)S(1)}, bf16[2,16,896]{2,1,0:T(8,128)(2,1)S(1)}, u32[]{:S(2)}, u32[]{:S(2)}) %collective-permute-start.20) | collective-permute-done | bytes 57376 | tf_op jit(solution)/shard_map/ppermute | solution.py:153
  46.6 1.9 %collective-permute-done.21.refs_2_ = bf16[2,16,896]{2,1,0:T(8,128)(2,1)S(1)} collective-permute-done((bf16[2,16,896]{2,1,0:T(8,128)(2,1)S(1)}, bf16[2,16,896]{2,1,0:T(8,128)(2,1)S(1)}, u32[]{:S(2)}, u32[]{:S(2)}) %collective-permute-start.21) | collective-permute-done | bytes 57376 | tf_op jit(solution)/shard_map/ppermute | solution.py:153
  48.6 0.6 %shard_map.140 = (bf16[16,896]{1,0:T(8,128)(2,1)}, bf16[16,896]{1,0:T(8,128)(2,1)}) custom-call(bf16[2,16,896]{2,1,0:T(8,128)(2,1)S(1)} %get-tuple-element.48.refs_0_, bf16[2,16,896]{2,1,0:T(8,128)(2,1)S(1)} %collective-permute-done.20.refs_1_, bf16[2,16,896]{2,1,0:T(8,128)(2,1)S(1)} %collective-permute-done.21.refs_2_, ...), custom_call_target="tpu_custom_call" | custom-call | tf_op jit(solution)/shard_map/pallas_call | solution.py:116
  (33 shorter events, 1.3 us)
Async XLA Ops:
  1.7 10.9 %collective-permute-start.3 = (bf16[16,7296]{1,0:T(8,128)(2,1)S(1)}, bf16[16,7296]{1,0:T(8,128)(2,1)S(1)}, u32[]{:S(2)}, u32[]{:S(2)}) collective-permute-start(bf16[16,7296]{1,0:T(8,128)(2,1)S(1)} %get-tuple-element.27.refs_0_), channel_id=1, source_target_pairs={{0,1},{1,0},{2,3},{3,2},{4,5},{5,4},{6,7},{7,6},{8,9},{9,8},{10,11... | collective-permute-start | bytes 700424 | tf_op jit(solution)/shard_map/ppermute | solution.py:153
  2.2 9.1 %collective-permute-start.2 = (bf16[16,1920]{1,0:T(8,128)(2,1)S(1)}, bf16[16,1920]{1,0:T(8,128)(2,1)S(1)}, u32[]{:S(2)}, u32[]{:S(2)}) collective-permute-start(bf16[16,1920]{1,0:T(8,128)(2,1)S(1)} %get-tuple-element.28._), channel_id=1, source_target_pairs={{0,6},{1,7},{2,4},{3,5},{4,2},{5,3},{6,0},{7,1},{8,14},{9,15},{10,... | collective-permute-start | bytes 184328 | tf_op jit(solution)/shard_map/ppermute | solution.py:153
  6.9 5.7 %collective-permute-start.1 = (bf16[16,1920]{1,0:T(8,128)(2,1)S(1)}, bf16[16,1920]{1,0:T(8,128)(2,1)S(1)}, u32[]{:S(2)}, u32[]{:S(2)}) collective-permute-start(bf16[16,1920]{1,0:T(8,128)(2,1)S(1)} %get-tuple-element.28._), channel_id=1, source_target_pairs={{0,4},{1,5},{2,6},{3,7},{4,0},{5,1},{6,2},{7,3},{8,12},{9,13},{10,... | collective-permute-start | bytes 184328 | tf_op jit(solution)/shard_map/ppermute | solution.py:153
  6.9 5.7 %collective-permute-start = (bf16[16,1920]{1,0:T(8,128)(2,1)S(1)}, bf16[16,1920]{1,0:T(8,128)(2,1)S(1)}, u32[]{:S(2)}, u32[]{:S(2)}) collective-permute-start(bf16[16,1920]{1,0:T(8,128)(2,1)S(1)} %get-tuple-element.28._), channel_id=1, source_target_pairs={{0,2},{1,3},{2,0},{3,1},{4,6},{5,7},{6,4},{7,5},{8,10},{9,11},{10,... | collective-permute-start | bytes 184328 | tf_op jit(solution)/shard_map/ppermute | solution.py:153
  12.7 5.3 %collective-permute-start.4 = (bf16[48,896]{1,0:T(8,128)(2,1)S(1)}, bf16[48,896]{1,0:T(8,128)(2,1)S(1)}, u32[]{:S(2)}, u32[]{:S(2)}) collective-permute-start(bf16[48,896]{1,0:T(8,128)(2,1)S(1)} %get-tuple-element.31.refs_0_), channel_id=1, source_target_pairs={{0,8},{1,17},{2,10},{3,19},{4,12},{5,21},{6,14},{7,23},{8,0},{9,25... | collective-permute-start | bytes 258056 | tf_op jit(solution)/shard_map/ppermute | solution.py:169
  14.2 7.5 %collective-permute-start.7 = (bf16[48,896]{1,0:T(8,128)(2,1)S(1)}, bf16[48,896]{1,0:T(8,128)(2,1)S(1)}, u32[]{:S(2)}, u32[]{:S(2)}) collective-permute-start(bf16[48,896]{1,0:T(8,128)(2,1)S(1)} %get-tuple-element.32), channel_id=1, source_target_pairs={{0,8},{8,0},{16,24},{24,16},{1,9},{9,1},{17,25},{25,17},{2,10},{10... | collective-permute-start | bytes 258056 | tf_op jit(solution)/shard_map/ppermute | solution.py:158
  14.8 7.0 %collective-permute-start.6 = (bf16[48,896]{1,0:T(8,128)(2,1)S(1)}, bf16[48,896]{1,0:T(8,128)(2,1)S(1)}, u32[]{:S(2)}, u32[]{:S(2)}) collective-permute-start(bf16[48,896]{1,0:T(8,128)(2,1)S(1)} %get-tuple-element.32), channel_id=1, source_target_pairs={{0,24},{8,16},{16,8},{24,0},{1,25},{9,17},{17,9},{25,1},{2,26},{10... | collective-permute-start | bytes 258056 | tf_op jit(solution)/shard_map/ppermute | solution.py:158
  17.2 5.1 %collective-permute-start.9 = (bf16[48,896]{1,0:T(8,128)(2,1)S(1)}, bf16[48,896]{1,0:T(8,128)(2,1)S(1)}, u32[]{:S(2)}, u32[]{:S(2)}) collective-permute-start(bf16[48,896]{1,0:T(8,128)(2,1)S(1)} %get-tuple-element.32), channel_id=1, source_target_pairs={{0,16},{8,24},{16,0},{24,8},{1,17},{9,25},{17,1},{25,9},{2,18},{10... | collective-permute-start | bytes 258056 | tf_op jit(solution)/shard_map/ppermute | solution.py:158
  17.7 4.6 %collective-permute-start.10 = (bf16[48,1920]{1,0:T(8,128)(2,1)S(1)}, bf16[48,1920]{1,0:T(8,128)(2,1)S(1)}, u32[]{:S(2)}, u32[]{:S(2)}) collective-permute-start(bf16[48,1920]{1,0:T(8,128)(2,1)S(1)} %get-tuple-element.30.refs_1_), channel_id=1, source_target_pairs={{0,1},{1,0},{2,3},{3,2},{4,5},{5,4},{6,7},{7,6},{8,9},{9,8},{10,11... | collective-permute-start | bytes 552968 | tf_op jit(solution)/shard_map/ppermute | solution.py:153
  18.0 6.1 %collective-permute-start.5 = (bf16[2,48,896]{2,1,0:T(8,128)(2,1)S(1)}, bf16[2,48,896]{2,1,0:T(8,128)(2,1)S(1)}, u32[]{:S(2)}, u32[]{:S(2)}) collective-permute-start(bf16[2,48,896]{2,1,0:T(8,128)(2,1)S(1)} %shard_map.125._), channel_id=1, source_target_pairs={{0,16},{1,9},{2,18},{3,11},{4,20},{5,13},{6,22},{7,15},{8,24},{9,1... | collective-permute-start | bytes 516104 | tf_op jit(solution)/shard_map/ppermute | solution.py:169
  21.7 2.4 %collective-permute-start.8 = (bf16[2,48,896]{2,1,0:T(8,128)(2,1)S(1)}, bf16[2,48,896]{2,1,0:T(8,128)(2,1)S(1)}, u32[]{:S(2)}, u32[]{:S(2)}) collective-permute-start(bf16[2,48,896]{2,1,0:T(8,128)(2,1)S(1)} %shard_map.127), channel_id=1, source_target_pairs={{0,1},{1,0},{2,3},{3,2},{4,5},{5,4},{6,7},{7,6},{8,9},{9,8},{10,11... | collective-permute-start | bytes 516104 | tf_op jit(solution)/shard_map/ppermute | solution.py:153
  22.3 1.8 %collective-permute-start.11 = (bf16[1,48,896]{2,1,0:T(8,128)(2,1)S(1)}, bf16[1,48,896]{2,1,0:T(8,128)(2,1)S(1)}, u32[]{:S(2)}, u32[]{:S(2)}) collective-permute-start(bf16[1,48,896]{2,1,0:T(8,128)(2,1)S(1)} %shard_map.128), channel_id=1, source_target_pairs={{0,1},{1,0},{2,3},{3,2},{4,5},{5,4},{6,7},{7,6},{8,9},{9,8},{10,11... | collective-permute-start | bytes 258056 | tf_op jit(solution)/shard_map/ppermute | solution.py:153
  24.1 2.4 %collective-permute-start.12 = (bf16[3,48,896]{2,1,0:T(8,128)(2,1)S(1)}, bf16[3,48,896]{2,1,0:T(8,128)(2,1)S(1)}, u32[]{:S(2)}, u32[]{:S(2)}) collective-permute-start(bf16[3,48,896]{2,1,0:T(8,128)(2,1)S(1)} %shard_map.129.refs_2_), channel_id=1, source_target_pairs={{0,1},{1,0},{2,3},{3,2},{4,5},{5,4},{6,7},{7,6},{8,9},{9,8},{10,11... | collective-permute-start | bytes 774152 | tf_op jit(solution)/shard_map/ppermute | solution.py:153
  26.0 2.4 %collective-permute-start.14 = (bf16[4,64,896]{2,1,0:T(8,128)(2,1)S(1)}, bf16[4,64,896]{2,1,0:T(8,128)(2,1)S(1)}, u32[]{:S(2)}, u32[]{:S(2)}) collective-permute-start(bf16[4,64,896]{2,1,0:T(8,128)(2,1)S(1)} %get-tuple-element.43), channel_id=1, source_target_pairs={{0,1},{1,0},{2,3},{3,2},{4,5},{5,4},{6,7},{7,6},{8,9},{9,8},{10,11... | collective-permute-start | bytes 1376264 | tf_op jit(solution)/shard_map/ppermute | solution.py:153
  28.3 1.9 %collective-permute-start.13 = (bf16[4,64,896]{2,1,0:T(8,128)(2,1)S(1)}, bf16[4,64,896]{2,1,0:T(8,128)(2,1)S(1)}, u32[]{:S(2)}, u32[]{:S(2)}) collective-permute-start(bf16[4,64,896]{2,1,0:T(8,128)(2,1)S(1)} %get-tuple-element.42), channel_id=1, source_target_pairs={{0,1},{1,0},{2,3},{3,2},{4,5},{5,4},{6,7},{7,6},{8,9},{9,8},{10,11... | collective-permute-start | bytes 1376264 | tf_op jit(solution)/shard_map/ppermute | solution.py:153
  28.5 4.9 %collective-permute-start.17 = (bf16[1,64,896]{2,1,0:T(8,128)(2,1)S(1)}, bf16[1,64,896]{2,1,0:T(8,128)(2,1)S(1)}, u32[]{:S(2)}, u32[]{:S(2)}) collective-permute-start(bf16[1,64,896]{2,1,0:T(8,128)(2,1)S(1)} %shard_map.137), channel_id=1, source_target_pairs={{0,16},{1,9},{2,18},{3,11},{4,20},{5,13},{6,22},{7,15},{8,24},{9,1... | collective-permute-start | bytes 344072 | tf_op jit(solution)/shard_map/ppermute | solution.py:169
  30.3 4.9 %collective-permute-start.15 = (bf16[1,64,896]{2,1,0:T(8,128)(2,1)S(1)}, bf16[1,64,896]{2,1,0:T(8,128)(2,1)S(1)}, u32[]{:S(2)}, u32[]{:S(2)}) collective-permute-start(bf16[1,64,896]{2,1,0:T(8,128)(2,1)S(1)} %shard_map.132._), channel_id=1, source_target_pairs={{0,16},{1,9},{2,18},{3,11},{4,20},{5,13},{6,22},{7,15},{8,24},{9,1... | collective-permute-start | bytes 344072 | tf_op jit(solution)/shard_map/ppermute | solution.py:169
  31.4 8.6 %collective-permute-start.19 = (bf16[2,64,896]{2,1,0:T(8,128)(2,1)S(1)}, bf16[2,64,896]{2,1,0:T(8,128)(2,1)S(1)}, u32[]{:S(2)}, u32[]{:S(2)}) collective-permute-start(bf16[2,64,896]{2,1,0:T(8,128)(2,1)S(1)} %shard_map.133.refs_2_), channel_id=1, source_target_pairs={{0,16},{1,9},{2,18},{3,11},{4,20},{5,13},{6,22},{7,15},{8,24},{9,1... | collective-permute-start | bytes 688136 | tf_op jit(solution)/shard_map/ppermute | solution.py:169
  33.4 4.9 %collective-permute-start.18 = (bf16[1,64,896]{2,1,0:T(8,128)(2,1)S(1)}, bf16[1,64,896]{2,1,0:T(8,128)(2,1)S(1)}, u32[]{:S(2)}, u32[]{:S(2)}) collective-permute-start(bf16[1,64,896]{2,1,0:T(8,128)(2,1)S(1)} %shard_map.138), channel_id=1, source_target_pairs={{0,8},{1,17},{2,10},{3,19},{4,12},{5,21},{6,14},{7,23},{8,0},{9,25... | collective-permute-start | bytes 344072 | tf_op jit(solution)/shard_map/ppermute | solution.py:169
  35.2 4.9 %collective-permute-start.16 = (bf16[1,64,896]{2,1,0:T(8,128)(2,1)S(1)}, bf16[1,64,896]{2,1,0:T(8,128)(2,1)S(1)}, u32[]{:S(2)}, u32[]{:S(2)}) collective-permute-start(bf16[1,64,896]{2,1,0:T(8,128)(2,1)S(1)} %shard_map.135), channel_id=1, source_target_pairs={{0,8},{1,17},{2,10},{3,19},{4,12},{5,21},{6,14},{7,23},{8,0},{9,25... | collective-permute-start | bytes 344072 | tf_op jit(solution)/shard_map/ppermute | solution.py:169
  40.1 6.5 %collective-permute-start.20 = (bf16[2,16,896]{2,1,0:T(8,128)(2,1)S(1)}, bf16[2,16,896]{2,1,0:T(8,128)(2,1)S(1)}, u32[]{:S(2)}, u32[]{:S(2)}) collective-permute-start(bf16[2,16,896]{2,1,0:T(8,128)(2,1)S(1)} %get-tuple-element.49), channel_id=1, source_target_pairs={{0,6},{1,7},{2,4},{3,5},{4,2},{5,3},{6,0},{7,1},{8,14},{9,15},{10,... | collective-permute-start | bytes 172040 | tf_op jit(solution)/shard_map/ppermute | solution.py:153
  42.5 6.1 %collective-permute-start.21 = (bf16[2,16,896]{2,1,0:T(8,128)(2,1)S(1)}, bf16[2,16,896]{2,1,0:T(8,128)(2,1)S(1)}, u32[]{:S(2)}, u32[]{:S(2)}) collective-permute-start(bf16[2,16,896]{2,1,0:T(8,128)(2,1)S(1)} %get-tuple-element.50), channel_id=1, source_target_pairs={{0,4},{1,5},{2,6},{3,7},{4,0},{5,1},{6,2},{7,3},{8,12},{9,13},{10,... | collective-permute-start | bytes 172040 | tf_op jit(solution)/shard_map/ppermute | solution.py:153
  42.7 5.8 %collective-permute-start.22 = (bf16[2,16,896]{2,1,0:T(8,128)(2,1)S(1)}, bf16[2,16,896]{2,1,0:T(8,128)(2,1)S(1)}, u32[]{:S(2)}, u32[]{:S(2)}) collective-permute-start(bf16[2,16,896]{2,1,0:T(8,128)(2,1)S(1)} %get-tuple-element.51), channel_id=1, source_target_pairs={{0,2},{1,3},{2,0},{3,1},{4,6},{5,7},{6,4},{7,5},{8,10},{9,11},{10,... | collective-permute-start | bytes 172040 | tf_op jit(solution)/shard_map/ppermute | solution.py:153

commit v3 on v2

--- a/solution.py
+++ b/solution.py
@@ -307,7 +307,7 @@
 
 
 def sent_order(sections):
-    return [sections - 1, *range(1, sections - 1)]
+    return [*range(1, sections - 2), sections - 1, sections - 2]
 
 
 def scale_column(m, experts, table_ref):

time: 49.4 us -> 49.5 us (level)
  starting transfers between devices: 23.2 us -> 24.8 us
  waiting for transfers between devices: 13.4 us -> 11.8 us
    ppermute x7, waiting for transfers between devices: 6.95 us -> 5.77 us  [swap_halves(): return lax.ppermute(x, ('section', 'expert'), pairs)]
    ppermute x7, starting transfers between devices: 8.48 us -> 9.35 us  [swap_halves(): return lax.ppermute(x, ('section', 'expert'), pairs)]
    ppermute x13, starting transfers between devices: 11.2 us -> 12 us  [swap_expert(): return lax.ppermute(x, 'expert', [(i, i ^ mask) for i in range(size)])]
  transfers between devices with their start and end apart: 23 -> 23, of which waited for: 11 -> 10; matrix products, arithmetic and copies ran while one was open for 0% -> 0% of each run, Pallas kernels for 20% -> 20%
where the time goes in v3:
time: 49.5 us; the launch traced here: 49.3 us
  starting transfers between devices  24.8 us (50%)
  Pallas kernels  11.9 us (24%)
  waiting for transfers between devices  11.8 us (24%)
  between operations  0.81 us (2%)
    ppermute x13, starting transfers between devices, swap_expert(): return lax.ppermute(x, 'expert', [(i, i ^ mask) for i in range(size)])  12 us
    pallas_call x19, Pallas kernels, call(): pl.pallas_call(kernel, out_shape=shapes, in_specs=[pl.BlockSpec(memory_sp...  11.9 us
    ppermute x7, starting transfers between devices, swap_halves(): return lax.ppermute(x, ('section', 'expert'), pairs)  9.35 us
    ppermute x13, waiting for transfers between devices, swap_expert(): return lax.ppermute(x, 'expert', [(i, i ^ mask) for i in range(size)])  6.05 us
    ppermute x7, waiting for transfers between devices, swap_halves(): return lax.ppermute(x, ('section', 'expert'), pairs)  5.77 us
    ppermute x3, starting transfers between devices, swap_section(): return lax.ppermute(x, 'section', [(i, i ^ mask) for i in range(size)])  3.49 us
  transfers between devices with their start and end apart: 23, of which 10 were waited for; matrix products, arithmetic and copies ran while one was open for 0% of the time, Pallas kernels for 20%

profile of v3, /device:TPU:0, one launch (start us, length us, event | category | flops | bytes accessed | tf_op | source)
XLA Modules:
  0.0 49.3 jit_solution(16123766084662343411)
XLA Ops:
  0.6 1.1 %shard_map.122 = (bf16[16,7296]{1,0:T(8,128)(2,1)S(1)}, bf16[16,1920]{1,0:T(8,128)(2,1)S(1)}) custom-call(bf16[16,3584]{1,0:T(8,128)(2,1)} %xa.1, s32[8,16]{1,0:T(8,128)} %bitcast.14, f32[8,16]{1,0:T(8,128)} %bitcast.15, bf16[16,3584]{1,0:T(8,128)(2,1)} %xb.1, s32[8,16]{1,0:T(8,128)} %bitcast.16, f32[8,16]{1,0:T(8,128)} %bitcast.17), custom_call_target="tpu_custom_call" | custom-call | tf_op jit(solution)/shard_map/pallas_call | solution.py:116
  1.7 0.5 %collective-permute-start.3 = (bf16[16,7296]{1,0:T(8,128)(2,1)S(1)}, bf16[16,7296]{1,0:T(8,128)(2,1)S(1)}, u32[]{:S(2)}, u32[]{:S(2)}) collective-permute-start(bf16[16,7296]{1,0:T(8,128)(2,1)S(1)} %get-tuple-element.27.refs_0_), channel_id=1, source_target_pairs={{0,1},{1,0},{2,3},{3,2},{4,5},{5,4},{6,7},{7,6},{8,9},{9,8},{10,11... | collective-permute-start | bytes 700424 | tf_op jit(solution)/shard_map/ppermute | solution.py:153
  2.2 4.7 %collective-permute-start.2 = (bf16[16,1920]{1,0:T(8,128)(2,1)S(1)}, bf16[16,1920]{1,0:T(8,128)(2,1)S(1)}, u32[]{:S(2)}, u32[]{:S(2)}) collective-permute-start(bf16[16,1920]{1,0:T(8,128)(2,1)S(1)} %get-tuple-element.28._), channel_id=1, source_target_pairs={{0,6},{1,7},{2,4},{3,5},{4,2},{5,3},{6,0},{7,1},{8,14},{9,15},{10,... | collective-permute-start | bytes 184328 | tf_op jit(solution)/shard_map/ppermute | solution.py:153
  6.9 0.6 %collective-permute-start = (bf16[16,1920]{1,0:T(8,128)(2,1)S(1)}, bf16[16,1920]{1,0:T(8,128)(2,1)S(1)}, u32[]{:S(2)}, u32[]{:S(2)}) collective-permute-start(bf16[16,1920]{1,0:T(8,128)(2,1)S(1)} %get-tuple-element.28._), channel_id=1, source_target_pairs={{0,2},{1,3},{2,0},{3,1},{4,6},{5,7},{6,4},{7,5},{8,10},{9,11},{10,... | collective-permute-start | bytes 184328 | tf_op jit(solution)/shard_map/ppermute | solution.py:153
  7.5 3.7 %shard_map.123 = (bf16[512,3584]{1,0:T(8,128)(2,1)S(1)}, bf16[3584,512]{1,0:T(8,128)(2,1)S(1)}, bf16[3584,512]{1,0:T(8,128)(2,1)S(1)}, bf16[512,3584]{1,0:T(8,12...) custom-call(bf16[512,3584]{1,0:T(8,128)(2,1)} %bitcast.9, bf16[3584,512]{1,0:T(8,128)(2,1)} %bitcast.10, ...), custom_call_target="tpu_custom_call" | custom-call | flops 1409286144 | bytes 11010048 | tf_op jit(solution)/shard_map/pallas_call | solution.py:116
  11.3 1.3 %collective-permute-done.1.refs_1_ = bf16[16,1920]{1,0:T(8,128)(2,1)S(1)} collective-permute-done((bf16[16,1920]{1,0:T(8,128)(2,1)S(1)}, bf16[16,1920]{1,0:T(8,128)(2,1)S(1)}, u32[]{:S(2)}, u32[]{:S(2)}) %collective-permute-start.1) | collective-permute-done | bytes 61472 | tf_op jit(solution)/shard_map/ppermute | solution.py:153
  12.7 1.6 %collective-permute-start.4 = (bf16[48,896]{1,0:T(8,128)(2,1)S(1)}, bf16[48,896]{1,0:T(8,128)(2,1)S(1)}, u32[]{:S(2)}, u32[]{:S(2)}) collective-permute-start(bf16[48,896]{1,0:T(8,128)(2,1)S(1)} %get-tuple-element.31.refs_0_), channel_id=1, source_target_pairs={{0,8},{1,17},{2,10},{3,19},{4,12},{5,21},{6,14},{7,23},{8,0},{9,25... | collective-permute-start | bytes 258056 | tf_op jit(solution)/shard_map/ppermute | solution.py:169
  14.2 1.5 %collective-permute-start.7 = (bf16[48,896]{1,0:T(8,128)(2,1)S(1)}, bf16[48,896]{1,0:T(8,128)(2,1)S(1)}, u32[]{:S(2)}, u32[]{:S(2)}) collective-permute-start(bf16[48,896]{1,0:T(8,128)(2,1)S(1)} %get-tuple-element.32), channel_id=1, source_target_pairs={{0,24},{8,16},{16,8},{24,0},{1,25},{9,17},{17,9},{25,1},{2,26},{10... | collective-permute-start | bytes 258056 | tf_op jit(solution)/shard_map/ppermute | solution.py:158
  15.7 1.5 %collective-permute-start.6 = (bf16[48,896]{1,0:T(8,128)(2,1)S(1)}, bf16[48,896]{1,0:T(8,128)(2,1)S(1)}, u32[]{:S(2)}, u32[]{:S(2)}) collective-permute-start(bf16[48,896]{1,0:T(8,128)(2,1)S(1)} %get-tuple-element.32), channel_id=1, source_target_pairs={{0,8},{8,0},{16,24},{24,16},{1,9},{9,1},{17,25},{25,17},{2,10},{10... | collective-permute-start | bytes 258056 | tf_op jit(solution)/shard_map/ppermute | solution.py:158
  17.2 0.5 %collective-permute-start.9 = (bf16[48,896]{1,0:T(8,128)(2,1)S(1)}, bf16[48,896]{1,0:T(8,128)(2,1)S(1)}, u32[]{:S(2)}, u32[]{:S(2)}) collective-permute-start(bf16[48,896]{1,0:T(8,128)(2,1)S(1)} %get-tuple-element.32), channel_id=1, source_target_pairs={{0,16},{8,24},{16,0},{24,8},{1,17},{9,25},{17,1},{25,9},{2,18},{10... | collective-permute-start | bytes 258056 | tf_op jit(solution)/shard_map/ppermute | solution.py:158
  17.7 0.3 collective-permute-done.4.refs_1_.refs_0_
  18.0 1.6 %collective-permute-start.5 = (bf16[2,48,896]{2,1,0:T(8,128)(2,1)S(1)}, bf16[2,48,896]{2,1,0:T(8,128)(2,1)S(1)}, u32[]{:S(2)}, u32[]{:S(2)}) collective-permute-start(bf16[2,48,896]{2,1,0:T(8,128)(2,1)S(1)} %shard_map.125._), channel_id=1, source_target_pairs={{0,16},{1,9},{2,18},{3,11},{4,20},{5,13},{6,22},{7,15},{8,24},{9,1... | collective-permute-start | bytes 516104 | tf_op jit(solution)/shard_map/ppermute | solution.py:169
  19.6 2.4 %shard_map.126 = (bf16[3584,512]{1,0:T(8,128)(2,1)S(1)}, bf16[512,3584]{1,0:T(8,128)(2,1)S(1)}) custom-call(bf16[3584,512]{1,0:T(8,128)(2,1)} %bitcast.11, bf16[2,48,896]{2,1,0:T(8,128)(2,1)S(1)} %shard_map.125._), custom_call_target="tpu_custom_call" | custom-call | flops 1000 | bytes 1000 | tf_op jit(solution)/shard_map/pallas_call | solution.py:116
  22.2 0.5 %collective-permute-start.11 = (bf16[1,48,896]{2,1,0:T(8,128)(2,1)S(1)}, bf16[1,48,896]{2,1,0:T(8,128)(2,1)S(1)}, u32[]{:S(2)}, u32[]{:S(2)}) collective-permute-start(bf16[1,48,896]{2,1,0:T(8,128)(2,1)S(1)} %shard_map.128), channel_id=1, source_target_pairs={{0,1},{1,0},{2,3},{3,2},{4,5},{5,4},{6,7},{7,6},{8,9},{9,8},{10,11... | collective-permute-start | bytes 258056 | tf_op jit(solution)/shard_map/ppermute | solution.py:153
  22.7 0.8 %collective-permute-done.5.refs_1_ = bf16[2,48,896]{2,1,0:T(8,128)(2,1)S(1)} collective-permute-done((bf16[2,48,896]{2,1,0:T(8,128)(2,1)S(1)}, bf16[2,48,896]{2,1,0:T(8,128)(2,1)S(1)}, u32[]{:S(2)}, u32[]{:S(2)}) %collective-permute-start.5) | collective-permute-done | bytes 172064 | tf_op jit(solution)/shard_map/ppermute | solution.py:169
  23.7 0.4 collective-permute-start.12
  24.1 1.8 %shard_map.130 = (bf16[4,64,896]{2,1,0:T(8,128)(2,1)S(1)}, bf16[4,64,896]{2,1,0:T(8,128)(2,1)S(1)}) custom-call(bf16[16,7296]{1,0:T(8,128)(2,1)S(1)} %get-tuple-element.27.refs_0_, bf16[48,1920]{1,0:T(8,128)(2,1)S(1)} %get-tuple-element.30.refs_1_, bf16[48,896]{1,0:T(8,128)(2,1)S(1)} %collective-permute-done.6.refs_0_.refs_2_, ...), custom_call_target="tpu_custom_call" | custom-call | flops 1000 | bytes 1000 | tf_op jit(solution)/shard_map/pallas_call | solution.py:116
  26.1 1.8 %shard_map.131 = (bf16[4,64,896]{2,1,0:T(8,128)(2,1)S(1)}, bf16[4,64,896]{2,1,0:T(8,128)(2,1)S(1)}) custom-call(bf16[16,7296]{1,0:T(8,128)(2,1)S(1)} %get-tuple-element.27.refs_0_, bf16[48,1920]{1,0:T(8,128)(2,1)S(1)} %get-tuple-element.30.refs_1_, bf16[3,48,896]{2,1,0:T(8,128)(2,1)S(1)} %shard_map.129.refs_2_, ...), custom_call_target="tpu_custom_call" | custom-call | flops 1000 | bytes 1000 | tf_op jit(solution)/shard_map/pallas_call | solution.py:116
  27.9 0.4 collective-permute-start.13
  28.3 1.1 %collective-permute-start.17 = (bf16[1,64,896]{2,1,0:T(8,128)(2,1)S(1)}, bf16[1,64,896]{2,1,0:T(8,128)(2,1)S(1)}, u32[]{:S(2)}, u32[]{:S(2)}) collective-permute-start(bf16[1,64,896]{2,1,0:T(8,128)(2,1)S(1)} %shard_map.137), channel_id=1, source_target_pairs={{0,16},{1,9},{2,18},{3,11},{4,20},{5,13},{6,22},{7,15},{8,24},{9,1... | collective-permute-start | bytes 344072 | tf_op jit(solution)/shard_map/ppermute | solution.py:169
  29.8 1.5 %collective-permute-start.15 = (bf16[1,64,896]{2,1,0:T(8,128)(2,1)S(1)}, bf16[1,64,896]{2,1,0:T(8,128)(2,1)S(1)}, u32[]{:S(2)}, u32[]{:S(2)}) collective-permute-start(bf16[1,64,896]{2,1,0:T(8,128)(2,1)S(1)} %shard_map.132._), channel_id=1, source_target_pairs={{0,16},{1,9},{2,18},{3,11},{4,20},{5,13},{6,22},{7,15},{8,24},{9,1... | collective-permute-start | bytes 344072 | tf_op jit(solution)/shard_map/ppermute | solution.py:169
  31.3 0.7 %collective-permute-start.19 = (bf16[2,64,896]{2,1,0:T(8,128)(2,1)S(1)}, bf16[2,64,896]{2,1,0:T(8,128)(2,1)S(1)}, u32[]{:S(2)}, u32[]{:S(2)}) collective-permute-start(bf16[2,64,896]{2,1,0:T(8,128)(2,1)S(1)} %shard_map.133.refs_2_), channel_id=1, source_target_pairs={{0,16},{1,9},{2,18},{3,11},{4,20},{5,13},{6,22},{7,15},{8,24},{9,1... | collective-permute-start | bytes 688136 | tf_op jit(solution)/shard_map/ppermute | solution.py:169
  32.1 1.1 %collective-permute-done.17.refs_1_ = bf16[1,64,896]{2,1,0:T(8,128)(2,1)S(1)} collective-permute-done((bf16[1,64,896]{2,1,0:T(8,128)(2,1)S(1)}, bf16[1,64,896]{2,1,0:T(8,128)(2,1)S(1)}, u32[]{:S(2)}, u32[]{:S(2)}) %collective-permute-start.17) | collective-permute-done | bytes 114720 | tf_op jit(solution)/shard_map/ppermute | solution.py:169
  33.2 1.6 %collective-permute-start.18 = (bf16[1,64,896]{2,1,0:T(8,128)(2,1)S(1)}, bf16[1,64,896]{2,1,0:T(8,128)(2,1)S(1)}, u32[]{:S(2)}, u32[]{:S(2)}) collective-permute-start(bf16[1,64,896]{2,1,0:T(8,128)(2,1)S(1)} %shard_map.138), channel_id=1, source_target_pairs={{0,8},{1,17},{2,10},{3,19},{4,12},{5,21},{6,14},{7,23},{8,0},{9,25... | collective-permute-start | bytes 344072 | tf_op jit(solution)/shard_map/ppermute | solution.py:169
  34.9 1.4 %collective-permute-start.16 = (bf16[1,64,896]{2,1,0:T(8,128)(2,1)S(1)}, bf16[1,64,896]{2,1,0:T(8,128)(2,1)S(1)}, u32[]{:S(2)}, u32[]{:S(2)}) collective-permute-start(bf16[1,64,896]{2,1,0:T(8,128)(2,1)S(1)} %shard_map.135), channel_id=1, source_target_pairs={{0,8},{1,17},{2,10},{3,19},{4,12},{5,21},{6,14},{7,23},{8,0},{9,25... | collective-permute-start | bytes 344072 | tf_op jit(solution)/shard_map/ppermute | solution.py:169
  36.3 1.8 %collective-permute-done.18.refs_3_ = bf16[1,64,896]{2,1,0:T(8,128)(2,1)S(1)} collective-permute-done((bf16[1,64,896]{2,1,0:T(8,128)(2,1)S(1)}, bf16[1,64,896]{2,1,0:T(8,128)(2,1)S(1)}, u32[]{:S(2)}, u32[]{:S(2)}) %collective-permute-start.18) | collective-permute-done | bytes 114720 | tf_op jit(solution)/shard_map/ppermute | solution.py:169
  38.1 1.7 %collective-permute-done.16.refs_1_ = bf16[1,64,896]{2,1,0:T(8,128)(2,1)S(1)} collective-permute-done((bf16[1,64,896]{2,1,0:T(8,128)(2,1)S(1)}, bf16[1,64,896]{2,1,0:T(8,128)(2,1)S(1)}, u32[]{:S(2)}, u32[]{:S(2)}) %collective-permute-start.16) | collective-permute-done | bytes 114720 | tf_op jit(solution)/shard_map/ppermute | solution.py:169
  39.9 2.6 %collective-permute-start.20 = (bf16[2,16,896]{2,1,0:T(8,128)(2,1)S(1)}, bf16[2,16,896]{2,1,0:T(8,128)(2,1)S(1)}, u32[]{:S(2)}, u32[]{:S(2)}) collective-permute-start(bf16[2,16,896]{2,1,0:T(8,128)(2,1)S(1)} %get-tuple-element.49), channel_id=1, source_target_pairs={{0,6},{1,7},{2,4},{3,5},{4,2},{5,3},{6,0},{7,1},{8,14},{9,15},{10,... | collective-permute-start | bytes 172040 | tf_op jit(solution)/shard_map/ppermute | solution.py:153
  42.8 1.5 %collective-permute-start.22 = (bf16[2,16,896]{2,1,0:T(8,128)(2,1)S(1)}, bf16[2,16,896]{2,1,0:T(8,128)(2,1)S(1)}, u32[]{:S(2)}, u32[]{:S(2)}) collective-permute-start(bf16[2,16,896]{2,1,0:T(8,128)(2,1)S(1)} %get-tuple-element.51), channel_id=1, source_target_pairs={{0,2},{1,3},{2,0},{3,1},{4,6},{5,7},{6,4},{7,5},{8,10},{9,11},{10,... | collective-permute-start | bytes 172040 | tf_op jit(solution)/shard_map/ppermute | solution.py:153
  44.3 2.1 %collective-permute-done.20.refs_1_ = bf16[2,16,896]{2,1,0:T(8,128)(2,1)S(1)} collective-permute-done((bf16[2,16,896]{2,1,0:T(8,128)(2,1)S(1)}, bf16[2,16,896]{2,1,0:T(8,128)(2,1)S(1)}, u32[]{:S(2)}, u32[]{:S(2)}) %collective-permute-start.20) | collective-permute-done | bytes 57376 | tf_op jit(solution)/shard_map/ppermute | solution.py:153
  46.4 2.3 %collective-permute-done.21.refs_2_ = bf16[2,16,896]{2,1,0:T(8,128)(2,1)S(1)} collective-permute-done((bf16[2,16,896]{2,1,0:T(8,128)(2,1)S(1)}, bf16[2,16,896]{2,1,0:T(8,128)(2,1)S(1)}, u32[]{:S(2)}, u32[]{:S(2)}) %collective-permute-start.21) | collective-permute-done | bytes 57376 | tf_op jit(solution)/shard_map/ppermute | solution.py:153
  48.7 0.6 %shard_map.140 = (bf16[16,896]{1,0:T(8,128)(2,1)}, bf16[16,896]{1,0:T(8,128)(2,1)}) custom-call(bf16[2,16,896]{2,1,0:T(8,128)(2,1)S(1)} %get-tuple-element.48.refs_0_, bf16[2,16,896]{2,1,0:T(8,128)(2,1)S(1)} %collective-permute-done.20.refs_1_, bf16[2,16,896]{2,1,0:T(8,128)(2,1)S(1)} %collective-permute-done.21.refs_2_, ...), custom_call_target="tpu_custom_call" | custom-call | tf_op jit(solution)/shard_map/pallas_call | solution.py:116
  (33 shorter events, 1.5 us)
Async XLA Ops:
  1.7 10.9 %collective-permute-start.3 = (bf16[16,7296]{1,0:T(8,128)(2,1)S(1)}, bf16[16,7296]{1,0:T(8,128)(2,1)S(1)}, u32[]{:S(2)}, u32[]{:S(2)}) collective-permute-start(bf16[16,7296]{1,0:T(8,128)(2,1)S(1)} %get-tuple-element.27.refs_0_), channel_id=1, source_target_pairs={{0,1},{1,0},{2,3},{3,2},{4,5},{5,4},{6,7},{7,6},{8,9},{9,8},{10,11... | collective-permute-start | bytes 700424 | tf_op jit(solution)/shard_map/ppermute | solution.py:153
  2.2 9.1 %collective-permute-start.2 = (bf16[16,1920]{1,0:T(8,128)(2,1)S(1)}, bf16[16,1920]{1,0:T(8,128)(2,1)S(1)}, u32[]{:S(2)}, u32[]{:S(2)}) collective-permute-start(bf16[16,1920]{1,0:T(8,128)(2,1)S(1)} %get-tuple-element.28._), channel_id=1, source_target_pairs={{0,6},{1,7},{2,4},{3,5},{4,2},{5,3},{6,0},{7,1},{8,14},{9,15},{10,... | collective-permute-start | bytes 184328 | tf_op jit(solution)/shard_map/ppermute | solution.py:153
  6.9 5.7 %collective-permute-start.1 = (bf16[16,1920]{1,0:T(8,128)(2,1)S(1)}, bf16[16,1920]{1,0:T(8,128)(2,1)S(1)}, u32[]{:S(2)}, u32[]{:S(2)}) collective-permute-start(bf16[16,1920]{1,0:T(8,128)(2,1)S(1)} %get-tuple-element.28._), channel_id=1, source_target_pairs={{0,4},{1,5},{2,6},{3,7},{4,0},{5,1},{6,2},{7,3},{8,12},{9,13},{10,... | collective-permute-start | bytes 184328 | tf_op jit(solution)/shard_map/ppermute | solution.py:153
  6.9 5.7 %collective-permute-start = (bf16[16,1920]{1,0:T(8,128)(2,1)S(1)}, bf16[16,1920]{1,0:T(8,128)(2,1)S(1)}, u32[]{:S(2)}, u32[]{:S(2)}) collective-permute-start(bf16[16,1920]{1,0:T(8,128)(2,1)S(1)} %get-tuple-element.28._), channel_id=1, source_target_pairs={{0,2},{1,3},{2,0},{3,1},{4,6},{5,7},{6,4},{7,5},{8,10},{9,11},{10,... | collective-permute-start | bytes 184328 | tf_op jit(solution)/shard_map/ppermute | solution.py:153
  12.7 5.4 %collective-permute-start.4 = (bf16[48,896]{1,0:T(8,128)(2,1)S(1)}, bf16[48,896]{1,0:T(8,128)(2,1)S(1)}, u32[]{:S(2)}, u32[]{:S(2)}) collective-permute-start(bf16[48,896]{1,0:T(8,128)(2,1)S(1)} %get-tuple-element.31.refs_0_), channel_id=1, source_target_pairs={{0,8},{1,17},{2,10},{3,19},{4,12},{5,21},{6,14},{7,23},{8,0},{9,25... | collective-permute-start | bytes 258056 | tf_op jit(solution)/shard_map/ppermute | solution.py:169
  14.2 7.8 %collective-permute-start.7 = (bf16[48,896]{1,0:T(8,128)(2,1)S(1)}, bf16[48,896]{1,0:T(8,128)(2,1)S(1)}, u32[]{:S(2)}, u32[]{:S(2)}) collective-permute-start(bf16[48,896]{1,0:T(8,128)(2,1)S(1)} %get-tuple-element.32), channel_id=1, source_target_pairs={{0,24},{8,16},{16,8},{24,0},{1,25},{9,17},{17,9},{25,1},{2,26},{10... | collective-permute-start | bytes 258056 | tf_op jit(solution)/shard_map/ppermute | solution.py:158
  15.7 6.3 %collective-permute-start.6 = (bf16[48,896]{1,0:T(8,128)(2,1)S(1)}, bf16[48,896]{1,0:T(8,128)(2,1)S(1)}, u32[]{:S(2)}, u32[]{:S(2)}) collective-permute-start(bf16[48,896]{1,0:T(8,128)(2,1)S(1)} %get-tuple-element.32), channel_id=1, source_target_pairs={{0,8},{8,0},{16,24},{24,16},{1,9},{9,1},{17,25},{25,17},{2,10},{10... | collective-permute-start | bytes 258056 | tf_op jit(solution)/shard_map/ppermute | solution.py:158
  17.2 4.9 %collective-permute-start.9 = (bf16[48,896]{1,0:T(8,128)(2,1)S(1)}, bf16[48,896]{1,0:T(8,128)(2,1)S(1)}, u32[]{:S(2)}, u32[]{:S(2)}) collective-permute-start(bf16[48,896]{1,0:T(8,128)(2,1)S(1)} %get-tuple-element.32), channel_id=1, source_target_pairs={{0,16},{8,24},{16,0},{24,8},{1,17},{9,25},{17,1},{25,9},{2,18},{10... | collective-permute-start | bytes 258056 | tf_op jit(solution)/shard_map/ppermute | solution.py:158
  17.7 4.4 %collective-permute-start.10 = (bf16[48,1920]{1,0:T(8,128)(2,1)S(1)}, bf16[48,1920]{1,0:T(8,128)(2,1)S(1)}, u32[]{:S(2)}, u32[]{:S(2)}) collective-permute-start(bf16[48,1920]{1,0:T(8,128)(2,1)S(1)} %get-tuple-element.30.refs_1_), channel_id=1, source_target_pairs={{0,1},{1,0},{2,3},{3,2},{4,5},{5,4},{6,7},{7,6},{8,9},{9,8},{10,11... | collective-permute-start | bytes 552968 | tf_op jit(solution)/shard_map/ppermute | solution.py:153
  18.0 5.5 %collective-permute-start.5 = (bf16[2,48,896]{2,1,0:T(8,128)(2,1)S(1)}, bf16[2,48,896]{2,1,0:T(8,128)(2,1)S(1)}, u32[]{:S(2)}, u32[]{:S(2)}) collective-permute-start(bf16[2,48,896]{2,1,0:T(8,128)(2,1)S(1)} %shard_map.125._), channel_id=1, source_target_pairs={{0,16},{1,9},{2,18},{3,11},{4,20},{5,13},{6,22},{7,15},{8,24},{9,1... | collective-permute-start | bytes 516104 | tf_op jit(solution)/shard_map/ppermute | solution.py:169
  22.1 1.5 %collective-permute-start.8 = (bf16[2,48,896]{2,1,0:T(8,128)(2,1)S(1)}, bf16[2,48,896]{2,1,0:T(8,128)(2,1)S(1)}, u32[]{:S(2)}, u32[]{:S(2)}) collective-permute-start(bf16[2,48,896]{2,1,0:T(8,128)(2,1)S(1)} %shard_map.127), channel_id=1, source_target_pairs={{0,1},{1,0},{2,3},{3,2},{4,5},{5,4},{6,7},{7,6},{8,9},{9,8},{10,11... | collective-permute-start | bytes 516104 | tf_op jit(solution)/shard_map/ppermute | solution.py:153
  22.2 1.5 %collective-permute-start.11 = (bf16[1,48,896]{2,1,0:T(8,128)(2,1)S(1)}, bf16[1,48,896]{2,1,0:T(8,128)(2,1)S(1)}, u32[]{:S(2)}, u32[]{:S(2)}) collective-permute-start(bf16[1,48,896]{2,1,0:T(8,128)(2,1)S(1)} %shard_map.128), channel_id=1, source_target_pairs={{0,1},{1,0},{2,3},{3,2},{4,5},{5,4},{6,7},{7,6},{8,9},{9,8},{10,11... | collective-permute-start | bytes 258056 | tf_op jit(solution)/shard_map/ppermute | solution.py:153
  23.7 2.4 %collective-permute-start.12 = (bf16[3,48,896]{2,1,0:T(8,128)(2,1)S(1)}, bf16[3,48,896]{2,1,0:T(8,128)(2,1)S(1)}, u32[]{:S(2)}, u32[]{:S(2)}) collective-permute-start(bf16[3,48,896]{2,1,0:T(8,128)(2,1)S(1)} %shard_map.129.refs_2_), channel_id=1, source_target_pairs={{0,1},{1,0},{2,3},{3,2},{4,5},{5,4},{6,7},{7,6},{8,9},{9,8},{10,11... | collective-permute-start | bytes 774152 | tf_op jit(solution)/shard_map/ppermute | solution.py:153
  25.9 2.4 %collective-permute-start.14 = (bf16[4,64,896]{2,1,0:T(8,128)(2,1)S(1)}, bf16[4,64,896]{2,1,0:T(8,128)(2,1)S(1)}, u32[]{:S(2)}, u32[]{:S(2)}) collective-permute-start(bf16[4,64,896]{2,1,0:T(8,128)(2,1)S(1)} %get-tuple-element.43), channel_id=1, source_target_pairs={{0,1},{1,0},{2,3},{3,2},{4,5},{5,4},{6,7},{7,6},{8,9},{9,8},{10,11... | collective-permute-start | bytes 1376264 | tf_op jit(solution)/shard_map/ppermute | solution.py:153
  27.9 1.9 %collective-permute-start.13 = (bf16[4,64,896]{2,1,0:T(8,128)(2,1)S(1)}, bf16[4,64,896]{2,1,0:T(8,128)(2,1)S(1)}, u32[]{:S(2)}, u32[]{:S(2)}) collective-permute-start(bf16[4,64,896]{2,1,0:T(8,128)(2,1)S(1)} %get-tuple-element.42), channel_id=1, source_target_pairs={{0,1},{1,0},{2,3},{3,2},{4,5},{5,4},{6,7},{7,6},{8,9},{9,8},{10,11... | collective-permute-start | bytes 1376264 | tf_op jit(solution)/shard_map/ppermute | solution.py:153
  28.3 4.9 %collective-permute-start.17 = (bf16[1,64,896]{2,1,0:T(8,128)(2,1)S(1)}, bf16[1,64,896]{2,1,0:T(8,128)(2,1)S(1)}, u32[]{:S(2)}, u32[]{:S(2)}) collective-permute-start(bf16[1,64,896]{2,1,0:T(8,128)(2,1)S(1)} %shard_map.137), channel_id=1, source_target_pairs={{0,16},{1,9},{2,18},{3,11},{4,20},{5,13},{6,22},{7,15},{8,24},{9,1... | collective-permute-start | bytes 344072 | tf_op jit(solution)/shard_map/ppermute | solution.py:169
  29.8 5.1 %collective-permute-start.15 = (bf16[1,64,896]{2,1,0:T(8,128)(2,1)S(1)}, bf16[1,64,896]{2,1,0:T(8,128)(2,1)S(1)}, u32[]{:S(2)}, u32[]{:S(2)}) collective-permute-start(bf16[1,64,896]{2,1,0:T(8,128)(2,1)S(1)} %shard_map.132._), channel_id=1, source_target_pairs={{0,16},{1,9},{2,18},{3,11},{4,20},{5,13},{6,22},{7,15},{8,24},{9,1... | collective-permute-start | bytes 344072 | tf_op jit(solution)/shard_map/ppermute | solution.py:169
  31.3 8.4 %collective-permute-start.19 = (bf16[2,64,896]{2,1,0:T(8,128)(2,1)S(1)}, bf16[2,64,896]{2,1,0:T(8,128)(2,1)S(1)}, u32[]{:S(2)}, u32[]{:S(2)}) collective-permute-start(bf16[2,64,896]{2,1,0:T(8,128)(2,1)S(1)} %shard_map.133.refs_2_), channel_id=1, source_target_pairs={{0,16},{1,9},{2,18},{3,11},{4,20},{5,13},{6,22},{7,15},{8,24},{9,1... | collective-permute-start | bytes 688136 | tf_op jit(solution)/shard_map/ppermute | solution.py:169
  33.2 4.9 %collective-permute-start.18 = (bf16[1,64,896]{2,1,0:T(8,128)(2,1)S(1)}, bf16[1,64,896]{2,1,0:T(8,128)(2,1)S(1)}, u32[]{:S(2)}, u32[]{:S(2)}) collective-permute-start(bf16[1,64,896]{2,1,0:T(8,128)(2,1)S(1)} %shard_map.138), channel_id=1, source_target_pairs={{0,8},{1,17},{2,10},{3,19},{4,12},{5,21},{6,14},{7,23},{8,0},{9,25... | collective-permute-start | bytes 344072 | tf_op jit(solution)/shard_map/ppermute | solution.py:169
  34.9 4.9 %collective-permute-start.16 = (bf16[1,64,896]{2,1,0:T(8,128)(2,1)S(1)}, bf16[1,64,896]{2,1,0:T(8,128)(2,1)S(1)}, u32[]{:S(2)}, u32[]{:S(2)}) collective-permute-start(bf16[1,64,896]{2,1,0:T(8,128)(2,1)S(1)} %shard_map.135), channel_id=1, source_target_pairs={{0,8},{1,17},{2,10},{3,19},{4,12},{5,21},{6,14},{7,23},{8,0},{9,25... | collective-permute-start | bytes 344072 | tf_op jit(solution)/shard_map/ppermute | solution.py:169
  39.9 6.5 %collective-permute-start.20 = (bf16[2,16,896]{2,1,0:T(8,128)(2,1)S(1)}, bf16[2,16,896]{2,1,0:T(8,128)(2,1)S(1)}, u32[]{:S(2)}, u32[]{:S(2)}) collective-permute-start(bf16[2,16,896]{2,1,0:T(8,128)(2,1)S(1)} %get-tuple-element.49), channel_id=1, source_target_pairs={{0,6},{1,7},{2,4},{3,5},{4,2},{5,3},{6,0},{7,1},{8,14},{9,15},{10,... | collective-permute-start | bytes 172040 | tf_op jit(solution)/shard_map/ppermute | solution.py:153
  42.5 6.1 %collective-permute-start.21 = (bf16[2,16,896]{2,1,0:T(8,128)(2,1)S(1)}, bf16[2,16,896]{2,1,0:T(8,128)(2,1)S(1)}, u32[]{:S(2)}, u32[]{:S(2)}) collective-permute-start(bf16[2,16,896]{2,1,0:T(8,128)(2,1)S(1)} %get-tuple-element.50), channel_id=1, source_target_pairs={{0,4},{1,5},{2,6},{3,7},{4,0},{5,1},{6,2},{7,3},{8,12},{9,13},{10,... | collective-permute-start | bytes 172040 | tf_op jit(solution)/shard_map/ppermute | solution.py:153
  42.8 5.8 %collective-permute-start.22 = (bf16[2,16,896]{2,1,0:T(8,128)(2,1)S(1)}, bf16[2,16,896]{2,1,0:T(8,128)(2,1)S(1)}, u32[]{:S(2)}, u32[]{:S(2)}) collective-permute-start(bf16[2,16,896]{2,1,0:T(8,128)(2,1)S(1)} %get-tuple-element.51), channel_id=1, source_target_pairs={{0,2},{1,3},{2,0},{3,1},{4,6},{5,7},{6,4},{7,5},{8,10},{9,11},{10,... | collective-permute-start | bytes 172040 | tf_op jit(solution)/shard_map/ppermute | solution.py:153
